TPU v7x, 32 devices: a whole 2x2x4 slice. The times are simulated.
32 devices in a mesh: groups: 2 (over y), dp: 16 (over z, x, core).
Axes of the slice: x: 2, y: 2, z: 4, core: 2. Of those that a mesh axis runs over, the one named last changes fastest.
Arguments:
- activations: bfloat16 [4096, 4096], P(('groups', 'dp')), parts along dimension 0
- gradients: bfloat16 [4096, 8, 1536], P(('groups', 'dp')), parts along dimension 0
- expert_ids: int32 [4096, 8], P(('groups', 'dp')), parts along dimension 0, may hold values from 0 to 127, all different within a row; in each aligned block of 128 rows (0 to 127, 128 to 255, ...) at most 16 rows name the same one
- window_experts: int32 [16], replicated, may hold values from 0 to 127, as said below
Outputs:
- input_factor: bfloat16 [131072, 4096], P(('groups', 'dp')), parts along dimension 0
- grad_factor: bfloat16 [49152, 1536], P(('groups', 'dp')), parts along dimension 0
There are 2 independent parts, one for each index of `groups`. A program takes and returns all parts, laid end to end along the dimension named above; an argument that names none is the same for every part. Nothing has to cross between parts.
Inputs may be any that keep to these rules, and one draw needn't show every extreme that they name: `expert_ids`: each token names 8 different experts; in each aligned block of 128 tokens no expert is named by more than 16 tokens. `window_experts`: 16 different experts.
All inputs are finite; a program needn't handle non-finite values.
Results may differ from a plain program's by a relative error of at most 0.001.
Values may be sent and summed in bfloat16 or wider, within the bound.
A program may use at most 256 MiB of HBM per device.

v0:
```python
import jax
import jax.numpy as jnp
from jax import lax
from jax.sharding import PartitionSpec as P

EXPERTS = 128
TOPK = 8
WIN = 16


damping_share = 1.0


def own_gram(rows, block_index, span):
    columns = lax.dynamic_slice_in_dim(rows, block_index * span, span, 1)
    return lax.dot_general(
        columns, rows, (((0,), (0,)), ((), ())), preferred_element_type=jnp.float32
    )


def diagonal_sum(gram_block, block_index):
    span = gram_block.shape[0]
    square = lax.dynamic_slice_in_dim(gram_block, block_index * span, span, 1)
    on_diagonal = jnp.arange(span)[:, None] == jnp.arange(span)[None, :]
    return jnp.sum(jnp.where(on_diagonal, square, 0.0))


def damped_block(gram_block, total, trace_value, block_index):
    span, width = gram_block.shape
    shift = damping_share * (trace_value / total) / width
    diagonal_mask = jnp.arange(span)[:, None] + block_index * span == jnp.arange(width)[None, :]
    return (gram_block / total + jnp.where(diagonal_mask, shift, 0.0)).astype(jnp.bfloat16)


def shards(activations, gradients, expert_ids, window_experts):
    devices = lax.axis_size("dp")
    group_size = devices // WIN
    tok_rows = activations.shape[0]
    block_rows = tok_rows // group_size
    slot_rows = max(2, 2 * block_rows * TOPK // EXPERTS)
    width_in = activations.shape[1]
    width_grad = gradients.shape[2]
    pair_rows = block_rows * TOPK
    matched = (expert_ids[:, :, None] == window_experts[None, None, :]).astype(jnp.int32)
    matched = matched.reshape(group_size, pair_rows, WIN)
    upper = (jnp.arange(pair_rows)[:, None] <= jnp.arange(pair_rows)[None, :]).astype(jnp.bfloat16)
    running = jnp.einsum(
        "gaw,ab->gbw", matched.astype(jnp.bfloat16), upper, preferred_element_type=jnp.float32
    )
    ordinal = running - 1.0
    placed = (matched[..., None] == 1) & (
        ordinal[..., None] == jnp.arange(slot_rows, dtype=jnp.float32)[None, None, None, :]
    )
    chosen = placed.astype(jnp.bfloat16)
    token_chosen = jnp.sum(chosen.reshape(group_size, block_rows, TOPK, WIN, slot_rows), axis=2)
    in_sorted = jnp.einsum(
        "gtws,gtd->wgsd",
        token_chosen,
        activations.reshape(group_size, block_rows, width_in),
        preferred_element_type=jnp.float32,
    ).astype(jnp.bfloat16)
    grad_sorted = jnp.einsum(
        "gaws,gaf->wgsf",
        chosen,
        gradients.reshape(group_size, pair_rows, width_grad),
        preferred_element_type=jnp.float32,
    ).astype(jnp.bfloat16)
    block_counts = jnp.sum(matched, axis=1).T.astype(jnp.bfloat16)
    copies_in = jnp.repeat(
        in_sorted.reshape(WIN, group_size * slot_rows, width_in), group_size, axis=0
    )
    copies_grad = jnp.repeat(
        grad_sorted.reshape(WIN, group_size * slot_rows, width_grad), group_size, axis=0
    )
    copies_count = jnp.repeat(block_counts, group_size, axis=0)
    arrived = (
        lax.all_to_all(copies_in, "dp", split_axis=0, concat_axis=0, tiled=True),
        lax.all_to_all(copies_grad, "dp", split_axis=0, concat_axis=0, tiled=True),
        lax.all_to_all(copies_count, "dp", split_axis=0, concat_axis=0, tiled=True),
    )
    in_rows = arrived[0].reshape(-1, width_in)
    grad_rows_all = arrived[1].reshape(-1, width_grad)
    total = jnp.sum(arrived[2].astype(jnp.float32))
    device_index = lax.axis_index("dp")
    block_index = device_index % group_size
    expert_slot = device_index // group_size
    gram_in = own_gram(in_rows, block_index, width_in // group_size)
    gram_grad = own_gram(grad_rows_all, block_index, width_grad // group_size)
    selector = (jnp.arange(WIN) == expert_slot).astype(jnp.float32)
    traces = lax.psum(
        (
            selector * diagonal_sum(gram_in, block_index),
            selector * diagonal_sum(gram_grad, block_index),
        ),
        "dp",
    )
    trace_in = jnp.sum(traces[0] * selector)
    trace_grad = jnp.sum(traces[1] * selector)
    return (
        damped_block(gram_in, total, trace_in, block_index),
        damped_block(gram_grad, total, trace_grad, block_index),
    )


def solution(mesh):
    placed = (
        P(("groups", "dp"), None),
        P(("groups", "dp"), None, None),
        P(("groups", "dp"), None),
        P(),
    )
    return jax.shard_map(
        shards,
        mesh=mesh,
        in_specs=placed,
        out_specs=(P(("groups", "dp"), None), P(("groups", "dp"), None)),
        check_vma=False,
    )
```

profile of v0, /device:TPU:0, one launch (start us, length us, event | category | flops | bytes accessed | tf_op | source)
XLA Modules:
  0.0 198.7 jit_solution(7506647527254171145)
XLA Ops:
  0.6 0.0 copy-start
  0.6 0.0 copy-start.1
  0.7 0.0 copy-start.2
  0.7 0.9 copy.17
  1.6 0.1 eq.156
  1.7 1.0 fusion.12
  2.7 0.7 convert_compare_fusion
  3.4 0.0 copy-done
  3.4 1.9 fusion.9
  5.3 7.4 %all-to-all-start.2 = ((bf16[16,16,1536]{2,1,0:T(8,128)(2,1)}), bf16[16,16,1536]{2,1,0:T(8,128)(2,1)}, u32[]{:S(2)}, u32[]{:S(2)}) async-start(bf16[16,16,1536]{2,1,0:T(8,128)(2,1)} %fusion.9), calls=%async_computation.2 | async-start | bytes 1572864 | tf_op jit(solution)/shard_map/all_to_all | solution.py:78
  12.7 1.0 copy.18
  13.7 1.2 copy.19
  14.9 0.0 copy-done.1
  14.9 0.0 copy-done.2
  14.9 0.1 convert_compare_fusion.1
  15.0 0.2 fusion.18
  15.3 3.2 %convolution_convert_fusion = bf16[16,16,4096]{2,1,0:T(8,128)(2,1)} fusion(bf16[128,16,16]{0,2,1:T(8,128)(2,1)S(1)} %fusion.18, bf16[128,4096]{1,0:T(8,128)(2,1)} %param.4), kind=kOutput, calls=%fused_computation.12 | convolution fusion | flops 269484032 | bytes 3211264 | tf_op jit(solution)/shard_map/gtws,gtd->wgsd/dot_general | solution.py:56
  18.5 13.0 %all-to-all-done.2 = bf16[16,16,1536]{2,1,0:T(8,128)(2,1)} async-done(((bf16[16,16,1536]{2,1,0:T(8,128)(2,1)}), bf16[16,16,1536]{2,1,0:T(8,128)(2,1)}, u32[]{:S(2)}, u32[]{:S(2)}) %all-to-all-start.2) | async-done | bytes 786464 | tf_op jit(solution)/shard_map/all_to_all | solution.py:78
  31.5 5.5 %all-to-all-start = ((bf16[16,16,4096]{2,1,0:T(8,128)(2,1)}), bf16[16,16,4096]{2,1,0:T(8,128)(2,1)}, u32[]{:S(2)}, u32[]{:S(2)}) async-start(bf16[16,16,4096]{2,1,0:T(8,128)(2,1)} %convolution_convert_fusion), calls=%async_computation | async-start | bytes 4194304 | tf_op jit(solution)/shard_map/all_to_all | solution.py:77
  37.0 0.2 convert_reduce_fusion
  37.2 0.7 copy.20
  37.9 7.2 %fusion.5 = (f32[]{:T(128)}, f32[1536,1536,1]{1,0,2:T(8,128)}) fusion(bf16[16,16,1536]{2,1,0:T(8,128)(2,1)} %all-to-all-done.2), kind=kOutput, calls=%fused_computation.10 | convolution fusion | flops 1215037440 | bytes 10223620 | tf_op jit(solution)/shard_map/dot_general | solution.py:16
  45.1 0.6 fusion.23
  45.8 32.4 %all-to-all-done = bf16[16,16,4096]{2,1,0:T(8,128)(2,1)} async-done(((bf16[16,16,4096]{2,1,0:T(8,128)(2,1)}), bf16[16,16,4096]{2,1,0:T(8,128)(2,1)}, u32[]{:S(2)}, u32[]{:S(2)}) %all-to-all-start) | async-done | bytes 2097184 | tf_op jit(solution)/shard_map/all_to_all | solution.py:77
  78.2 11.2 %all-to-all-start.1 = ((bf16[16,1,1]{2,1,0:T(2,128)(2,1)}), bf16[16,1,1]{2,1,0:T(2,128)(2,1)S(1)}, u32[]{:S(2)}, u32[]{:S(2)}) async-start(bf16[16,1,1]{2,1,0:T(2,128)(2,1)} %copy.20), calls=%async_computation.1 | async-start | bytes 16384 | tf_op jit(solution)/shard_map/all_to_all | solution.py:79
  89.4 29.7 %fusion.2 = (f32[]{:T(128)}, f32[4096,4096,1]{1,0,2:T(8,128)}) fusion(bf16[16,16,4096]{2,1,0:T(8,128)(2,1)} %all-to-all-done), kind=kOutput, calls=%fused_computation.4 | convolution fusion | flops 8640266240 | bytes 69206016 | tf_op jit(solution)/shard_map/dot_general | solution.py:16
  119.1 0.6 fusion.24
  119.8 0.0 all-to-all-done.1
  119.8 0.6 convert_reduce_fusion.1
  120.4 33.8 %all-reduce = (f32[16]{0:T(128)S(1)}, f32[16]{0:T(128)S(1)}) all-reduce(f32[16]{0:T(128)S(1)} %fusion.24, f32[16]{0:T(128)S(1)} %fusion.23), channel_id=1, replica_groups=mesh['groups'=2,'dp'=16] {'dp'}, use_global_device_ids=true, to_apply=%region_4.5 | all-reduce | flops 32 | bytes 256 | tf_op jit(solution)/shard_map/psum | solution.py:90
  154.2 0.7 select_reduce_fusion
  157.5 7.7 %fusion.4 = bf16[1536,1536]{1,0:T(8,128)(2,1)} fusion(f32[1536,1536,1]{1,0,2:T(8,128)} %get-tuple-element.7, f32[]{:T(128)S(6)} %div.33, f32[]{:T(128)} %convert_reduce_fusion.1), kind=kLoop, calls=%fused_computation.9 | loop fusion | flops 11796480 | bytes 14155784 | tf_op jit(solution)/shard_map/convert_element_type | solution.py:32
  165.1 33.5 %fusion.1 = bf16[4096,4096]{1,0:T(8,128)(2,1)} fusion(f32[4096,4096,1]{1,0,2:T(8,128)} %get-tuple-element.5, f32[]{:T(128)S(6)} %div.29, f32[]{:T(128)} %convert_reduce_fusion.1), kind=kLoop, calls=%fused_computation.3 | loop fusion | flops 83886080 | bytes 100663304 | tf_op jit(solution)/shard_map/convert_element_type | solution.py:32
  (1 shorter events, 0.0 us)
Async XLA Ops:
  0.6 2.8 %copy-start = (bf16[128,8,1536]{2,1,0:T(8,128)(2,1)S(1)}, bf16[128,8,1536]{2,1,0:T(8,128)(2,1)}, u32[]{:S(2)}) copy-start(bf16[128,8,1536]{2,1,0:T(8,128)(2,1)} %param.5) | copy-start | bytes 9437188
  0.6 14.3 %copy-start.1 = (s32[128,8]{0,1:T(8,128)S(1)}, s32[128,8]{0,1:T(8,128)}, u32[]{:S(2)}) copy-start(s32[128,8]{0,1:T(8,128)} %param.6) | copy-start | bytes 12292
  0.7 14.3 %copy-start.2 = (s32[16]{0:T(128)S(1)}, s32[16]{0:T(128)}, u32[]{:S(2)}) copy-start(s32[16]{0:T(128)} %param.7) | copy-start | bytes 196
  5.3 26.2 %all-to-all-start.2 = ((bf16[16,16,1536]{2,1,0:T(8,128)(2,1)}), bf16[16,16,1536]{2,1,0:T(8,128)(2,1)}, u32[]{:S(2)}, u32[]{:S(2)}) async-start(bf16[16,16,1536]{2,1,0:T(8,128)(2,1)} %fusion.9), calls=%async_computation.2 | async-start | bytes 1572864 | tf_op jit(solution)/shard_map/all_to_all | solution.py:78
  31.5 46.7 %all-to-all-start = ((bf16[16,16,4096]{2,1,0:T(8,128)(2,1)}), bf16[16,16,4096]{2,1,0:T(8,128)(2,1)}, u32[]{:S(2)}, u32[]{:S(2)}) async-start(bf16[16,16,4096]{2,1,0:T(8,128)(2,1)} %convolution_convert_fusion), calls=%async_computation | async-start | bytes 4194304 | tf_op jit(solution)/shard_map/all_to_all | solution.py:77
  78.2 41.6 %all-to-all-start.1 = ((bf16[16,1,1]{2,1,0:T(2,128)(2,1)}), bf16[16,1,1]{2,1,0:T(2,128)(2,1)S(1)}, u32[]{:S(2)}, u32[]{:S(2)}) async-start(bf16[16,1,1]{2,1,0:T(2,128)(2,1)} %copy.20), calls=%async_computation.1 | async-start | bytes 16384 | tf_op jit(solution)/shard_map/all_to_all | solution.py:79
where the time goes:
time: 199 us
  waiting for transfers between devices  45.4 us (23%)
  other arithmetic  45 us (23%)
  matrix products  43 us (22%)
  blocking collectives  33.8 us (17%)
  starting transfers between devices  24.1 us (12%)
  local copies, waits for them, and re-layouts  3.95 us (2%)
  between operations  3.3 us (2%)
    convert_element_type x2, other arithmetic, damped_block(): (gram_block / total + jnp.where(diagonal_mask, shift, 0.0)).astype(jnp.bf...  41.2 us
    dot_general x2, matrix products, own_gram(): lax.dot_general(columns, rows, (((0,), (0,)), ((), ())), preferred_elemen...  36.9 us
    psum x1, blocking collectives, shards(): lax.psum((selector * diagonal_sum(gram_in, block_index), selector * diago...  33.8 us
    all_to_all x1, waiting for transfers between devices, shards(): lax.all_to_all(copies_in, 'dp', split_axis=0, concat_axis=0, tiled=True)  32.4 us
    all_to_all x1, waiting for transfers between devices, shards(): lax.all_to_all(copies_grad, 'dp', split_axis=0, concat_axis=0, tiled=True)  13 us
    all_to_all x1, starting transfers between devices, shards(): lax.all_to_all(copies_count, 'dp', split_axis=0, concat_axis=0, tiled=True)  11.2 us
    all_to_all x1, starting transfers between devices, shards(): lax.all_to_all(copies_grad, 'dp', split_axis=0, concat_axis=0, tiled=True)  7.4 us
    all_to_all x1, starting transfers between devices, shards(): lax.all_to_all(copies_in, 'dp', split_axis=0, concat_axis=0, tiled=True)  5.53 us
  transfers between devices with their start and end apart: 3, of which 2 were waited for; matrix products, arithmetic and copies ran while one was open for 23% of the time, Pallas kernels for 0%

commit v1 on v0

v1 whole, which is shorter than its diff:
```python
import functools

import jax
import jax.numpy as jnp
from jax import lax
from jax.experimental import pallas as pl
from jax.experimental.pallas import tpu as pltpu
from jax.sharding import PartitionSpec as P

EXPERTS = 128
TOPK = 8
WIN = 16
FLAG = 128


damping_share = 1.0


def row_tile(span):
    for tile in (512, 256, 128):
        if span % tile == 0:
            return tile
    return span


def factor_kernel(width, tile, chunk, aligned, start_ref, total_ref, left_ref, rows_ref, out_ref, shift_ref):
    step = pl.program_id(0)
    depth = rows_ref.shape[0]
    inverse = 1.0 / total_ref[0]

    @pl.when(step == 0)
    def _():
        def add(i, sums):
            part = rows_ref[pl.ds(pl.multiple_of(i * 16, 16), 16), :width].astype(jnp.float32)
            return sums + part * part

        sums = lax.fori_loop(0, depth // 16, add, jnp.zeros((16, width), jnp.float32))
        shift_ref[0] = damping_share * jnp.sum(sums) * inverse / width

    left = left_ref[...]
    dims = (((0,), (0,)), ((), ()))

    def scaled(columns):
        part = lax.dot_general(left, rows_ref[:, columns], dims, preferred_element_type=jnp.float32)
        return part * inverse

    def damped(value, first_row, first_column):
        down = lax.broadcasted_iota(jnp.int32, value.shape, 0) + first_row
        across = lax.broadcasted_iota(jnp.int32, value.shape, 1) + first_column
        return value + jnp.where(down == across, shift_ref[0], 0.0)

    first_row = start_ref[0] + step * tile
    for column in range(0, width, chunk):
        columns = pl.ds(column, chunk)
        value = scaled(columns)
        if not aligned:
            value = damped(value, first_row, column)
        out_ref[:, columns] = value.astype(jnp.bfloat16)
    if aligned:
        columns = pl.ds(pl.multiple_of(step * tile, tile), tile)
        out_ref[:, columns] = damped(scaled(columns), 0, 0).astype(jnp.bfloat16)


def factor(rows, width, total, block_index, group_size, name):
    depth = rows.shape[0]
    span = width // group_size
    tile = row_tile(span)
    aligned = group_size == 1
    left = rows if aligned else lax.dynamic_slice_in_dim(rows, block_index * span, span, 1)
    return pl.pallas_call(
        functools.partial(factor_kernel, width, tile, 512, aligned),
        out_shape=jax.ShapeDtypeStruct((span, width), jnp.bfloat16),
        grid=(span // tile,),
        in_specs=[
            pl.BlockSpec(memory_space=pltpu.SMEM),
            pl.BlockSpec(memory_space=pltpu.SMEM),
            pl.BlockSpec((depth, tile), lambda i: (0, i)),
            pl.BlockSpec(rows.shape, lambda i: (0, 0)),
        ],
        out_specs=pl.BlockSpec((tile, width), lambda i: (i, 0)),
        scratch_shapes=[pltpu.SMEM((1,), jnp.float32)],
        compiler_params=pltpu.CompilerParams(vmem_limit_bytes=56 * 1024 * 1024),
        cost_estimate=pl.CostEstimate(
            flops=2 * depth * span * width, bytes_accessed=2 * span * width + 2 * depth * width, transcendentals=0
        ),
        name=name,
    )((block_index * span).astype(jnp.int32).reshape(1), total.reshape(1), left, rows)


def shards(activations, gradients, expert_ids, window_experts):
    devices = lax.axis_size("dp")
    group_size = devices // WIN
    tok_rows = activations.shape[0]
    block_rows = tok_rows // group_size
    slot_rows = max(2, 2 * block_rows * TOPK // EXPERTS)
    width_in = activations.shape[1]
    width_grad = gradients.shape[2]
    pair_rows = block_rows * TOPK
    matched = (expert_ids[:, :, None] == window_experts[None, None, :]).astype(jnp.int32)
    matched = matched.reshape(group_size, pair_rows, WIN)
    upper = (jnp.arange(pair_rows)[:, None] <= jnp.arange(pair_rows)[None, :]).astype(jnp.bfloat16)
    running = jnp.einsum(
        "gaw,ab->gbw", matched.astype(jnp.bfloat16), upper, preferred_element_type=jnp.float32
    )
    ordinal = running - 1.0
    placed = (matched[..., None] == 1) & (
        ordinal[..., None] == jnp.arange(slot_rows, dtype=jnp.float32)[None, None, None, :]
    )
    chosen = placed.astype(jnp.bfloat16)
    token_chosen = jnp.sum(chosen.reshape(group_size, block_rows, TOPK, WIN, slot_rows), axis=2)
    in_sorted = jnp.einsum(
        "gtws,gtd->wgsd",
        token_chosen,
        activations.reshape(group_size, block_rows, width_in),
        preferred_element_type=jnp.float32,
    ).astype(jnp.bfloat16)
    grad_sorted = jnp.einsum(
        "gaws,gaf->wgsf",
        chosen,
        gradients.reshape(group_size, pair_rows, width_grad),
        preferred_element_type=jnp.float32,
    ).astype(jnp.bfloat16)
    flags = jnp.sum(token_chosen, axis=1).transpose(1, 0, 2)[..., None]
    in_sorted = jnp.concatenate(
        [in_sorted, jnp.broadcast_to(flags, in_sorted.shape[:3] + (FLAG,))], axis=3
    )
    copies_in = jnp.repeat(
        in_sorted.reshape(WIN, group_size * slot_rows, width_in + FLAG), group_size, axis=0
    )
    copies_grad = jnp.repeat(
        grad_sorted.reshape(WIN, group_size * slot_rows, width_grad), group_size, axis=0
    )
    in_rows = lax.all_to_all(copies_in, "dp", split_axis=0, concat_axis=0, tiled=True)
    grad_rows = lax.all_to_all(copies_grad, "dp", split_axis=0, concat_axis=0, tiled=True)
    in_rows = in_rows.reshape(-1, width_in + FLAG)
    grad_rows = grad_rows.reshape(-1, width_grad)
    total = jnp.sum(in_rows[:, width_in].astype(jnp.float32))
    block_index = lax.axis_index("dp") % group_size
    return (
        factor(in_rows, width_in, total, block_index, group_size, "input_factor"),
        factor(grad_rows, width_grad, total, block_index, group_size, "grad_factor"),
    )


def solution(mesh):
    placed = (
        P(("groups", "dp"), None),
        P(("groups", "dp"), None, None),
        P(("groups", "dp"), None),
        P(),
    )
    return jax.shard_map(
        shards,
        mesh=mesh,
        in_specs=placed,
        out_specs=(P(("groups", "dp"), None), P(("groups", "dp"), None)),
        check_vma=False,
    )
```

time: 199 us -> 97.8 us (0.49)
  other arithmetic: 45 us -> 4.18 us
  matrix products: 43 us -> 4.79 us
  blocking collectives: 33.8 us -> 0 us
  Pallas kernels: 0 us -> 24.9 us
  waiting for transfers between devices: 45.4 us -> 40.3 us
  starting transfers between devices: 24.1 us -> 19.1 us
  between operations: 3.3 us -> 0.71 us
    convert_element_type x3 -> x0, other arithmetic: 41.2 us -> none  [the longest x2 41.2 us: damped_block(): (gram_block / total + jnp.where(diagonal_mask, shift, 0.0)).astype(jnp.bf...]
    dot_general x2 -> x0, matrix products: 36.9 us -> none  [own_gram(): lax.dot_general(columns, rows, (((0,), (0,)), ((), ())), preferred_elemen...]
    psum x1 -> x0, blocking collectives: 33.8 us -> none  [shards(): lax.psum((selector * diagonal_sum(gram_in, block_index), selector * diago...]
    pallas_call x0 -> x2, Pallas kernels: none -> 24.9 us  [factor(): pl.pallas_call(functools.partial(factor_kernel, width, tile, 512, aligned...]
    all_to_all x1, waiting for transfers between devices: 13 us -> 0.01 us  [shards(): lax.all_to_all(copies_grad, 'dp', split_axis=0, concat_axis=0, tiled=True)]
    all_to_all x1 -> x0, starting transfers between devices: 11.2 us -> none  [shards(): lax.all_to_all(copies_count, 'dp', split_axis=0, concat_axis=0, tiled=True)]
    all_to_all x1, waiting for transfers between devices: 32.4 us -> 40.3 us  [shards(): lax.all_to_all(copies_in, 'dp', split_axis=0, concat_axis=0, tiled=True)]
    all_to_all x1, starting transfers between devices: 7.4 us -> 11.5 us  [shards(): lax.all_to_all(copies_grad, 'dp', split_axis=0, concat_axis=0, tiled=True)]
  transfers between devices with their start and end apart: 3 -> 2, of which waited for: 2 -> 1; matrix products, arithmetic and copies ran while one was open for 23% -> 4% of each run, Pallas kernels for 0% -> 19%
where the time goes in v1:
time: 97.8 us; the launch traced here: 97.3 us
  waiting for transfers between devices  40.3 us (41%)
  Pallas kernels  24.9 us (25%)
  starting transfers between devices  19.1 us (20%)
  matrix products  4.79 us (5%)
  other arithmetic  4.18 us (4%)
  local copies, waits for them, and re-layouts  3.34 us (3%)
    all_to_all x1, waiting for transfers between devices, shards(): lax.all_to_all(copies_in, 'dp', split_axis=0, concat_axis=0, tiled=True)  40.3 us
    pallas_call x2, Pallas kernels, factor(): pl.pallas_call(functools.partial(factor_kernel, width, tile, 512, aligned...  24.9 us
    all_to_all x1, starting transfers between devices, shards(): lax.all_to_all(copies_grad, 'dp', split_axis=0, concat_axis=0, tiled=True)  11.5 us
    all_to_all x1, starting transfers between devices, shards(): lax.all_to_all(copies_in, 'dp', split_axis=0, concat_axis=0, tiled=True)  7.53 us
  transfers between devices with their start and end apart: 2, of which 1 were waited for; matrix products, arithmetic and copies ran while one was open for 4% of the time, Pallas kernels for 19%

profile of v1, /device:TPU:0, one launch (start us, length us, event | category | flops | bytes accessed | tf_op | source)
XLA Modules:
  0.0 97.3 jit_solution(561516501269404877)
XLA Ops:
  0.6 0.0 copy-start
  0.6 0.9 copy.11
  1.6 0.1 eq.85
  1.7 0.8 convert_compare_fusion.1
  2.5 1.0 %fusion.7 = f32[1024,16]{0,1:T(8,128)S(1)} fusion(s32[1024]{0:T(1024)S(1)} %eq.85, s32[16]{0:T(128)} %param.7), kind=kOutput, calls=%fused_computation.8 | convolution fusion | flops 34668544 | bytes 69696 | tf_op jit(solution)/shard_map/gaw,ab->gbw/dot_general | solution.py:102
  3.4 1.0 %copy.12 = f32[1024,16]{1,0:T(8,128)} copy(f32[1024,16]{0,1:T(8,128)S(1)} %fusion.7) | data formatting | bytes 131072 | tf_op jit(solution)/shard_map/sub | solution.py:105
  4.4 1.2 %copy.13 = f32[128,8,16]{0,2,1:T(8,128)S(1)} copy(f32[128,8,16]{2,1,0:T(8,128)} %bitcast.23) | data formatting | bytes 131072 | tf_op jit(solution)/shard_map/eq | solution.py:107
  5.6 0.3 fusion.14
  5.9 1.9 %fusion = bf16[16,1,16,4096]{3,2,0,1:T(8,128)(2,1)S(1)} fusion(bf16[128,16,16]{0,2,1:T(8,128)(2,1)S(1)} %get-tuple-element.2, bf16[128,4096]{1,0:T(8,128)(2,1)} %param.4), kind=kOutput, calls=%fused_computation.1 | convolution fusion | flops 269484032 | bytes 3211264 | tf_op jit(solution)/shard_map/gtws,gtd->wgsd/dot_general | solution.py:111
  7.9 0.1 broadcast_in_dim.2
  8.0 1.5 %maximum_bitcast_fusion = bf16[16,16,4224]{2,1,0:T(8,128)(2,1)} fusion(bf16[16,1,16,128]{3,2,0,1:T(8,128)(2,1)S(1)} %broadcast_in_dim.2, bf16[16,1,16,4096]{3,2,0,1:T(8,128)(2,1)S(1)} %fusion), kind=kLoop, calls=%fused_computation.7 | loop fusion | flops 4325376 | bytes 4325376 | tf_op jit(solution)/shard_map/reshape;broadcast_in_dim;reshape | solution.py:127
  9.5 0.0 copy-start.1
  9.5 7.5 %all-to-all-start = ((bf16[16,16,4224]{2,1,0:T(8,128)(2,1)}), bf16[16,16,4224]{2,1,0:T(8,128)(2,1)}, u32[]{:S(2)}, u32[]{:S(2)}) async-start(bf16[16,16,4224]{2,1,0:T(8,128)(2,1)} %maximum_bitcast_fusion), calls=%async_computation | async-start | bytes 4325376 | tf_op jit(solution)/shard_map/all_to_all | solution.py:133
  17.0 0.0 copy-done.1
  17.0 0.1 convert_compare_fusion
  17.1 0.0 copy-done
  17.1 1.9 %fusion.4 = bf16[16,16,1536]{2,1,0:T(8,128)(2,1)} fusion(bf16[128,8,1536]{2,1,0:T(8,128)(2,1)S(1)} %copy-done, f32[1024,16]{0,1:T(8,128)S(1)} %fusion.7, pred[1024,16]{0,1:T(8,128)(4,1)S(1)} %convert_compare_fusion), kind=kOutput, calls=%fused_computation.6 | convolution fusion | flops 806223872 | bytes 4014080 | tf_op jit(solution)/shard_map/gaws,gaf->wgsf/dot_general | solution.py:117
  19.0 40.3 %all-to-all-done = bf16[16,16,4224]{2,1,0:T(8,128)(2,1)} async-done(((bf16[16,16,4224]{2,1,0:T(8,128)(2,1)}), bf16[16,16,4224]{2,1,0:T(8,128)(2,1)}, u32[]{:S(2)}, u32[]{:S(2)}) %all-to-all-start) | async-done | bytes 2162720 | tf_op jit(solution)/shard_map/all_to_all | solution.py:133
  59.3 11.5 %all-to-all-start.1 = ((bf16[16,16,1536]{2,1,0:T(8,128)(2,1)}), bf16[16,16,1536]{2,1,0:T(8,128)(2,1)}, u32[]{:S(2)}, u32[]{:S(2)}) async-start(bf16[16,16,1536]{2,1,0:T(8,128)(2,1)} %fusion.4), calls=%async_computation.1 | async-start | bytes 1572864 | tf_op jit(solution)/shard_map/all_to_all | solution.py:134
  70.9 1.5 %convert_reduce_fusion = f32[]{:T(128)} fusion(bf16[256,4224]{1,0:T(8,128)(2,1)} %bitcast.6.left_ref.rows_ref), kind=kLoop, calls=%fused_computation.19 | loop fusion | flops 511 | bytes 516 | tf_op jit(solution)/shard_map/reduce_sum | solution.py:137
  72.4 18.8 %input_factor.1 = bf16[4096,4096]{1,0:T(8,128)(2,1)} custom-call(s32[1]{0:T(128)} %constant.24.clone.1.start_ref, f32[1]{0:T(128)} %bitcast.7.total_ref, bf16[256,4224]{1,0:T(8,128)(2,1)} %bitcast.6.left_ref.rows_ref, bf16[256,4224]{1,0:T(8,128)(2,1)} %bitcast.6.left_ref.rows_ref), custom_call_target="tpu_custom_call" | custom-call | flops 8589934592 | bytes 35651584 | tf_op jit(solution)/shard_map/input_factor/pallas_call | solution.py:70
  91.2 0.0 all-to-all-done.1
  91.2 6.1 %grad_factor.1 = bf16[1536,1536]{1,0:T(8,128)(2,1)} custom-call(s32[1]{0:T(128)} %constant.24.clone.1.start_ref, f32[1]{0:T(128)} %bitcast.7.total_ref, bf16[256,1536]{1,0:T(8,128)(2,1)} %bitcast.10.left_ref.rows_ref, bf16[256,1536]{1,0:T(8,128)(2,1)} %bitcast.10.left_ref.rows_ref), custom_call_target="tpu_custom_call" | custom-call | flops 1207959552 | bytes 5505024 | tf_op jit(solution)/shard_map/grad_factor/pallas_call | solution.py:70
Async XLA Ops:
  0.6 16.5 %copy-start = (bf16[128,8,1536]{2,1,0:T(8,128)(2,1)S(1)}, bf16[128,8,1536]{2,1,0:T(8,128)(2,1)}, u32[]{:S(2)}) copy-start(bf16[128,8,1536]{2,1,0:T(8,128)(2,1)} %param.5) | copy-start | bytes 9437188
  9.5 7.5 %copy-start.1 = (s32[16]{0:T(128)S(1)}, s32[16]{0:T(128)}, u32[]{:S(2)}) copy-start(s32[16]{0:T(128)} %param.7) | copy-start | bytes 196
  9.5 49.8 %all-to-all-start = ((bf16[16,16,4224]{2,1,0:T(8,128)(2,1)}), bf16[16,16,4224]{2,1,0:T(8,128)(2,1)}, u32[]{:S(2)}, u32[]{:S(2)}) async-start(bf16[16,16,4224]{2,1,0:T(8,128)(2,1)} %maximum_bitcast_fusion), calls=%async_computation | async-start | bytes 4325376 | tf_op jit(solution)/shard_map/all_to_all | solution.py:133
  59.3 31.9 %all-to-all-start.1 = ((bf16[16,16,1536]{2,1,0:T(8,128)(2,1)}), bf16[16,16,1536]{2,1,0:T(8,128)(2,1)}, u32[]{:S(2)}, u32[]{:S(2)}) async-start(bf16[16,16,1536]{2,1,0:T(8,128)(2,1)} %fusion.4), calls=%async_computation.1 | async-start | bytes 1572864 | tf_op jit(solution)/shard_map/all_to_all | solution.py:134

commit v2 on v1

v2 whole, which is shorter than its diff:
```python
import functools

import jax
import jax.numpy as jnp
from jax import lax
from jax.experimental import pallas as pl
from jax.experimental.pallas import tpu as pltpu
from jax.sharding import PartitionSpec as P

EXPERTS = 128
TOPK = 8
WIN = 16
FLAG = 128


damping_share = 1.0


def row_tile(span):
    for tile in (512, 256, 128):
        if span % tile == 0:
            return tile
    return span


def factor_kernel(width, tile, chunk, aligned, start_ref, flags_ref, left_ref, rows_ref, out_ref, scale_ref):
    step = pl.program_id(0)
    depth = rows_ref.shape[0]
    piece = min(depth, 128)

    @pl.when(step == 0)
    def _():
        def add(i, sums):
            rows = pl.ds(pl.multiple_of(i * piece, piece), piece)
            out = []
            for column, before in zip(range(0, width, chunk), sums):
                part = rows_ref[rows, column:column + chunk].astype(jnp.float32)
                out.append(before + jnp.sum((part * part).reshape(piece // 8, 8, chunk), axis=0))
            return out

        zeros = [jnp.zeros((8, chunk), jnp.float32)] * (width // chunk)
        sums = lax.fori_loop(0, depth // piece, add, zeros)
        whole = functools.reduce(lambda x, y: x + y, sums)
        inverse = FLAG / jnp.sum(flags_ref[...].astype(jnp.float32))
        scale_ref[0] = inverse
        scale_ref[1] = damping_share * jnp.sum(whole) * inverse / width

    inverse = scale_ref[0]
    left = left_ref[...].T

    def scaled(block, columns):
        return jnp.dot(block, rows_ref[:, columns], preferred_element_type=jnp.float32) * inverse

    def damped(value, first_row, first_column):
        down = lax.broadcasted_iota(jnp.int32, value.shape, 0) + first_row
        across = lax.broadcasted_iota(jnp.int32, value.shape, 1) + first_column
        return value + jnp.where(down == across, scale_ref[1], 0.0)

    first_row = start_ref[0] + step * tile
    for column in range(0, width, chunk):
        columns = pl.ds(column, chunk)
        value = scaled(left, columns)
        if not aligned:
            value = damped(value, first_row, column)
        out_ref[:, columns] = value.astype(jnp.bfloat16)
    if aligned:
        side = min(tile, 256)
        for down in range(0, tile, side):
            columns = pl.ds(pl.multiple_of(step * tile + down, side), side)
            value = damped(scaled(left[down:down + side], columns), 0, 0)
            out_ref[pl.ds(down, side), columns] = value.astype(jnp.bfloat16)


def select_kernel(block_rows, slot_rows, ids_ref, window_ref, act_ref, out_ref):
    tokens, width = act_ref.shape
    per_expert = tokens // block_rows * slot_rows
    rows = WIN * per_expert

    def iota(shape, dim):
        return lax.broadcasted_iota(jnp.int32, shape, dim)

    ids, window = ids_ref[...], window_ref[...]
    matched = jnp.zeros((tokens, WIN), jnp.float32)
    for k in range(ids.shape[1]):
        matched += jnp.where(ids[:, k:k + 1] == window, 1.0, 0.0)
    matched = matched.astype(jnp.bfloat16)
    later, earlier = iota((tokens, tokens), 0), iota((tokens, tokens), 1)
    before = (earlier < later) & (earlier // block_rows == later // block_rows)
    place = jnp.dot(
        jnp.where(before, 1.0, 0.0).astype(jnp.bfloat16), matched, preferred_element_type=jnp.float32
    ).astype(jnp.bfloat16)
    spread = jnp.where(iota((rows, WIN), 0) // per_expert == iota((rows, WIN), 1), 1.0, 0.0).astype(jnp.bfloat16)
    dims = (((1,), (1,)), ((), ()))
    hit = lax.dot_general(spread, matched, dims, preferred_element_type=jnp.float32)
    position = lax.dot_general(spread, place, dims, preferred_element_type=jnp.float32)
    row, token = iota((rows, tokens), 0), iota((rows, tokens), 1)
    inside = row % per_expert
    taken = (
        (hit > 0.5)
        & (position.astype(jnp.int32) == inside % slot_rows)
        & (token // block_rows == inside // slot_rows)
    )
    chosen = jnp.where(taken, 1.0, 0.0)
    flags = jnp.sum(chosen, axis=1, keepdims=True)
    out_ref[:, width:] = jnp.broadcast_to(flags, (rows, FLAG)).astype(jnp.bfloat16)
    chosen = chosen.astype(jnp.bfloat16)
    for column in range(0, width, 512):
        columns = pl.ds(column, 512)
        out_ref[:, columns] = jnp.dot(
            chosen, act_ref[:, columns], preferred_element_type=jnp.float32
        ).astype(jnp.bfloat16)


def select_rows(expert_ids, window_experts, activations, block_rows, slot_rows):
    tokens, width = activations.shape
    per_expert = tokens // block_rows * slot_rows
    return pl.pallas_call(
        functools.partial(select_kernel, block_rows, slot_rows),
        out_shape=jax.ShapeDtypeStruct((WIN * per_expert, width + FLAG), jnp.bfloat16),
        in_specs=[pl.BlockSpec(memory_space=pltpu.VMEM)] * 3,
        out_specs=pl.BlockSpec(memory_space=pltpu.VMEM),
        compiler_params=pltpu.CompilerParams(vmem_limit_bytes=32 * 1024 * 1024),
        cost_estimate=pl.CostEstimate(
            flops=2 * WIN * per_expert * tokens * width, bytes_accessed=6 * tokens * width, transcendentals=0
        ),
        name="select_rows",
    )(expert_ids, window_experts.reshape(1, WIN), activations)


def factor(rows, width, flagged, block_index, group_size, name):
    depth = rows.shape[0]
    span = width // group_size
    tile = row_tile(span)
    aligned = group_size == 1
    left = rows if aligned else lax.dynamic_slice_in_dim(rows, block_index * span, span, 1)
    return pl.pallas_call(
        functools.partial(factor_kernel, width, tile, 512, aligned),
        out_shape=jax.ShapeDtypeStruct((span, width), jnp.bfloat16),
        grid=(span // tile,),
        in_specs=[
            pl.BlockSpec(memory_space=pltpu.SMEM),
            pl.BlockSpec((depth, FLAG), lambda i: (0, flagged.shape[1] // FLAG - 1)),
            pl.BlockSpec((depth, tile), lambda i: (0, i)),
            pl.BlockSpec(rows.shape, lambda i: (0, 0)),
        ],
        out_specs=pl.BlockSpec((tile, width), lambda i: (i, 0)),
        scratch_shapes=[pltpu.SMEM((2,), jnp.float32)],
        compiler_params=pltpu.CompilerParams(vmem_limit_bytes=56 * 1024 * 1024),
        cost_estimate=pl.CostEstimate(
            flops=2 * depth * span * width, bytes_accessed=2 * span * width + 2 * depth * width, transcendentals=0
        ),
        name=name,
    )((block_index * span).astype(jnp.int32).reshape(1), flagged, left, rows)


def shards(activations, gradients, expert_ids, window_experts):
    devices = lax.axis_size("dp")
    group_size = devices // WIN
    tok_rows = activations.shape[0]
    block_rows = tok_rows // group_size
    slot_rows = max(2, 2 * block_rows * TOPK // EXPERTS)
    width_in = activations.shape[1]
    width_grad = gradients.shape[2]
    pair_rows = block_rows * TOPK
    matched = (expert_ids[:, :, None] == window_experts[None, None, :]).astype(jnp.int32)
    matched = matched.reshape(group_size, pair_rows, WIN)
    upper = (jnp.arange(pair_rows)[:, None] <= jnp.arange(pair_rows)[None, :]).astype(jnp.bfloat16)
    running = jnp.einsum(
        "gaw,ab->gbw", matched.astype(jnp.bfloat16), upper, preferred_element_type=jnp.float32
    )
    ordinal = running - 1.0
    placed = (matched[..., None] == 1) & (
        ordinal[..., None] == jnp.arange(slot_rows, dtype=jnp.float32)[None, None, None, :]
    )
    chosen = placed.astype(jnp.bfloat16)
    in_sorted = select_rows(expert_ids, window_experts, activations, block_rows, slot_rows)
    grad_sorted = jnp.einsum(
        "gaws,gaf->wgsf",
        chosen,
        gradients.reshape(group_size, pair_rows, width_grad),
        preferred_element_type=jnp.float32,
    ).astype(jnp.bfloat16)
    copies_in = jnp.repeat(
        in_sorted.reshape(WIN, group_size * slot_rows, width_in + FLAG), group_size, axis=0
    )
    copies_grad = jnp.repeat(
        grad_sorted.reshape(WIN, group_size * slot_rows, width_grad), group_size, axis=0
    )
    in_rows = lax.all_to_all(copies_in, "dp", split_axis=0, concat_axis=0, tiled=True)
    grad_rows = lax.all_to_all(copies_grad, "dp", split_axis=0, concat_axis=0, tiled=True)
    in_rows = in_rows.reshape(-1, width_in + FLAG)
    grad_rows = grad_rows.reshape(-1, width_grad)
    block_index = lax.axis_index("dp") % group_size
    return (
        factor(in_rows, width_in, in_rows, block_index, group_size, "input_factor"),
        factor(grad_rows, width_grad, in_rows, block_index, group_size, "grad_factor"),
    )


def solution(mesh):
    placed = (
        P(("groups", "dp"), None),
        P(("groups", "dp"), None, None),
        P(("groups", "dp"), None),
        P(),
    )
    return jax.shard_map(
        shards,
        mesh=mesh,
        in_specs=placed,
        out_specs=(P(("groups", "dp"), None), P(("groups", "dp"), None)),
        check_vma=False,
    )
```

time: 97.8 us -> 91.7 us (0.938)
  other arithmetic: 4.18 us -> 0.08 us
  matrix products: 4.79 us -> 2.23 us
  Pallas kernels: 24.9 us -> 23.4 us
  waiting for transfers between devices: 40.3 us -> 41.6 us
    unnamed x5 -> x11, local copies, waits for them, and re-layouts: 0.95 us -> 4.18 us
    pallas_call x2, Pallas kernels: 24.9 us -> 22.2 us  [factor(): pl.pallas_call(functools.partial(factor_kernel, width, tile, 512, aligned...]
    dot_general x1 -> x0, matrix products: 1.94 us -> none  [shards(): jnp.einsum('gtws,gtd->wgsd', token_chosen, activations.reshape(group_size...]
    reduce_sum x2 -> x0, other arithmetic: 1.83 us -> none  [the longest x1 1.54 us: shards(): total = jnp.sum(in_rows[:, width_in].astype(jnp.float32))]
    all_to_all x1, waiting for transfers between devices: 0.01 us -> 1.75 us  [shards(): lax.all_to_all(copies_grad, 'dp', split_axis=0, concat_axis=0, tiled=True)]
    another operation x1 -> x0, other arithmetic: 1.5 us -> none  [shards(): jnp.repeat(in_sorted.reshape(WIN, group_size * slot_rows, width_in + FLAG...]
    pallas_call x0 -> x1, Pallas kernels: none -> 1.25 us  [select_rows(): pl.pallas_call(functools.partial(select_kernel, block_rows, slot_rows), o...]
    eq x1 -> x0, local copies, waits for them, and re-layouts: 1.2 us -> none  [shards(): ordinal[..., None]]
  transfers between devices with their start and end apart: 2 -> 2, of which waited for: 1 -> 2; matrix products, arithmetic and copies ran while one was open for 4% -> 3% of each run, Pallas kernels for 19% -> 19%
where the time goes in v2:
time: 91.7 us; the launch traced here: 91.3 us
  waiting for transfers between devices  41.6 us (45%)
  Pallas kernels  23.4 us (26%)
  starting transfers between devices  18.9 us (21%)
  local copies, waits for them, and re-layouts  4.27 us (5%)
  matrix products  2.23 us (2%)
    all_to_all x1, waiting for transfers between devices, shards(): lax.all_to_all(copies_in, 'dp', split_axis=0, concat_axis=0, tiled=True)  39.9 us
    pallas_call x2, Pallas kernels, factor(): pl.pallas_call(functools.partial(factor_kernel, width, tile, 512, aligned...  22.2 us
    all_to_all x1, starting transfers between devices, shards(): lax.all_to_all(copies_grad, 'dp', split_axis=0, concat_axis=0, tiled=True)  11.5 us
    all_to_all x1, starting transfers between devices, shards(): lax.all_to_all(copies_in, 'dp', split_axis=0, concat_axis=0, tiled=True)  7.4 us
    unnamed x11, local copies, waits for them, and re-layouts  4.18 us
    dot_general x1, matrix products, shards(): jnp.einsum('gaws,gaf->wgsf', chosen, gradients.reshape(group_size, pair_r...  1.9 us
  transfers between devices with their start and end apart: 2, of which 2 were waited for; matrix products, arithmetic and copies ran while one was open for 3% of the time, Pallas kernels for 19%

profile of v2, /device:TPU:0, one launch (start us, length us, event | category | flops | bytes accessed | tf_op | source)
XLA Modules:
  0.0 91.3 jit_solution(14674062228772523767)
XLA Ops:
  0.6 0.0 copy-start
  0.6 0.9 %copy.7.ids_ref = s32[128,8]{1,0:T(8,128)S(1)} copy(s32[128,8]{0,1:T(8,128)} %param.6) | data formatting | bytes 8192 | tf_op args[2]
  1.6 0.0 copy-start.2
  1.6 1.2 %copy-done.2 = bf16[128,4096]{1,0:T(8,128)(2,1)S(1)} copy-done((bf16[128,4096]{1,0:T(8,128)(2,1)S(1)}, bf16[128,4096]{1,0:T(8,128)(2,1)}, u32[]{:S(2)}) %copy-start.2) | copy-done | bytes 1048600
  2.8 0.0 copy-start.3
  2.8 0.7 copy-done.3
  3.5 0.0 copy-start.4
  3.5 1.2 %select_rows.1 = bf16[256,4224]{1,0:T(8,128)(2,1)S(1)} custom-call(s32[128,8]{1,0:T(8,128)S(1)} %copy.7.ids_ref, s32[1,16]{1,0:T(1,128)S(1)} %bitcast.12, bf16[128,4096]{1,0:T(8,128)(2,1)S(1)} %copy-done.2), custom_call_target="tpu_custom_call" | custom-call | flops 268435456 | bytes 3145728 | tf_op jit(solution)/shard_map/select_rows/pallas_call | solution.py:117
  4.7 0.0 copy-start.1
  4.7 1.3 %copy-done.1 = bf16[256,4224]{1,0:T(8,128)(2,1)} copy-done((bf16[256,4224]{1,0:T(8,128)(2,1)}, bf16[256,4224]{1,0:T(8,128)(2,1)S(1)}, u32[]{:S(2)}) %copy-start.1) | copy-done | bytes 2162712
  6.1 7.4 %all-to-all-start = ((bf16[16,16,4224]{2,1,0:T(8,128)(2,1)}), bf16[16,16,4224]{2,1,0:T(8,128)(2,1)}, u32[]{:S(2)}, u32[]{:S(2)}) async-start(bf16[16,16,4224]{2,1,0:T(8,128)(2,1)} %bitcast.11), calls=%async_computation | async-start | bytes 4325376 | tf_op jit(solution)/shard_map/all_to_all | solution.py:189
  13.5 0.1 eq.52
  13.6 0.0 copy-done.4
  13.6 0.1 convert_compare_fusion
  13.7 0.3 fusion.6
  14.0 0.0 copy-done
  14.0 1.9 %fusion.3 = bf16[16,16,1536]{2,1,0:T(8,128)(2,1)} fusion(bf16[128,8,1536]{2,1,0:T(8,128)(2,1)S(1)} %copy-done, f32[1024,16]{0,1:T(8,128)S(1)} %fusion.6, pred[1024,16]{0,1:T(8,128)(4,1)S(1)} %convert_compare_fusion), kind=kOutput, calls=%fused_computation.4 | convolution fusion | flops 806223872 | bytes 4014080 | tf_op jit(solution)/shard_map/gaws,gaf->wgsf/dot_general | solution.py:177
  15.9 39.9 %all-to-all-done = bf16[16,16,4224]{2,1,0:T(8,128)(2,1)} async-done(((bf16[16,16,4224]{2,1,0:T(8,128)(2,1)}), bf16[16,16,4224]{2,1,0:T(8,128)(2,1)}, u32[]{:S(2)}, u32[]{:S(2)}) %all-to-all-start) | async-done | bytes 2162720 | tf_op jit(solution)/shard_map/all_to_all | solution.py:189
  55.8 11.5 %all-to-all-start.1 = ((bf16[16,16,1536]{2,1,0:T(8,128)(2,1)}), bf16[16,16,1536]{2,1,0:T(8,128)(2,1)}, u32[]{:S(2)}, u32[]{:S(2)}) async-start(bf16[16,16,1536]{2,1,0:T(8,128)(2,1)} %fusion.3), calls=%async_computation.1 | async-start | bytes 1572864 | tf_op jit(solution)/shard_map/all_to_all | solution.py:190
  67.3 17.0 %input_factor.1 = bf16[4096,4096]{1,0:T(8,128)(2,1)} custom-call(s32[1]{0:T(128)} %constant.21.clone.1.start_ref, bf16[256,4224]{1,0:T(8,128)(2,1)} %bitcast.2.flags_ref.left_ref.rows_ref, bf16[256,4224]{1,0:T(8,128)(2,1)} %bitcast.2.flags_ref.left_ref.rows_ref, bf16[256,4224]{1,0:T(8,128)(2,1)} %bitcast.2.flags_ref.left_ref.rows_ref), custom_call_target="tpu_custom_call" | custom-call | flops 8589934592 | bytes 35651584 | tf_op jit(solution)/shard_map/input_factor/pallas_call | solution.py:136
  84.3 1.7 %all-to-all-done.1 = bf16[16,16,1536]{2,1,0:T(8,128)(2,1)} async-done(((bf16[16,16,1536]{2,1,0:T(8,128)(2,1)}), bf16[16,16,1536]{2,1,0:T(8,128)(2,1)}, u32[]{:S(2)}, u32[]{:S(2)}) %all-to-all-start.1) | async-done | bytes 786464 | tf_op jit(solution)/shard_map/all_to_all | solution.py:190
  86.1 5.2 %grad_factor.1 = bf16[1536,1536]{1,0:T(8,128)(2,1)} custom-call(s32[1]{0:T(128)} %constant.21.clone.1.start_ref, bf16[256,4224]{1,0:T(8,128)(2,1)} %bitcast.2.flags_ref.left_ref.rows_ref, bf16[256,1536]{1,0:T(8,128)(2,1)} %bitcast.5.left_ref.rows_ref, bf16[256,1536]{1,0:T(8,128)(2,1)} %bitcast.5.left_ref.rows_ref), custom_call_target="tpu_custom_call" | custom-call | flops 1207959552 | bytes 5505024 | tf_op jit(solution)/shard_map/grad_factor/pallas_call | solution.py:136
Async XLA Ops:
  0.6 13.4 %copy-start = (bf16[128,8,1536]{2,1,0:T(8,128)(2,1)S(1)}, bf16[128,8,1536]{2,1,0:T(8,128)(2,1)}, u32[]{:S(2)}) copy-start(bf16[128,8,1536]{2,1,0:T(8,128)(2,1)} %param.5) | copy-start | bytes 9437188
  1.6 1.2 %copy-start.2 = (bf16[128,4096]{1,0:T(8,128)(2,1)S(1)}, bf16[128,4096]{1,0:T(8,128)(2,1)}, u32[]{:S(2)}) copy-start(bf16[128,4096]{1,0:T(8,128)(2,1)} %act_ref.1) | copy-start | bytes 3145732
  2.8 0.7 copy-start.3
  3.5 10.1 %copy-start.4 = (s32[16]{0:T(128)S(1)}, s32[16]{0:T(128)}, u32[]{:S(2)}) copy-start(s32[16]{0:T(128)} %param.7) | copy-start | bytes 196
  4.7 1.3 %copy-start.1 = (bf16[256,4224]{1,0:T(8,128)(2,1)}, bf16[256,4224]{1,0:T(8,128)(2,1)S(1)}, u32[]{:S(2)}) copy-start(bf16[256,4224]{1,0:T(8,128)(2,1)S(1)} %select_rows.1) | copy-start | bytes 6488068
  6.1 49.7 %all-to-all-start = ((bf16[16,16,4224]{2,1,0:T(8,128)(2,1)}), bf16[16,16,4224]{2,1,0:T(8,128)(2,1)}, u32[]{:S(2)}, u32[]{:S(2)}) async-start(bf16[16,16,4224]{2,1,0:T(8,128)(2,1)} %bitcast.11), calls=%async_computation | async-start | bytes 4325376 | tf_op jit(solution)/shard_map/all_to_all | solution.py:189
  55.8 30.3 %all-to-all-start.1 = ((bf16[16,16,1536]{2,1,0:T(8,128)(2,1)}), bf16[16,16,1536]{2,1,0:T(8,128)(2,1)}, u32[]{:S(2)}, u32[]{:S(2)}) async-start(bf16[16,16,1536]{2,1,0:T(8,128)(2,1)} %fusion.3), calls=%async_computation.1 | async-start | bytes 1572864 | tf_op jit(solution)/shard_map/all_to_all | solution.py:190

commit v3 on v2

--- a/solution.py
+++ b/solution.py
@@ -16,9 +16,9 @@
 damping_share = 1.0
 
 
-def row_tile(span):
-    for tile in (512, 256, 128):
-        if span % tile == 0:
+def row_tile(span, width):
+    for tile in (512, 256):
+        if span % tile == 0 and tile * 4 <= max(width, 1024):
             return tile
     return span
 
@@ -130,7 +130,7 @@
 def factor(rows, width, flagged, block_index, group_size, name):
     depth = rows.shape[0]
     span = width // group_size
-    tile = row_tile(span)
+    tile = row_tile(span, width)
     aligned = group_size == 1
     left = rows if aligned else lax.dynamic_slice_in_dim(rows, block_index * span, span, 1)
     return pl.pallas_call(

time: 91.7 us -> 93.3 us (1.017)
  Pallas kernels: 23.4 us -> 25 us
    pallas_call x2, Pallas kernels: 22.2 us -> 23.8 us  [factor(): pl.pallas_call(functools.partial(factor_kernel, width, tile, 512, aligned...]
  transfers between devices with their start and end apart: 2 -> 2, of which waited for: 2 -> 2; matrix products, arithmetic and copies ran while one was open for 3% -> 3% of each run, Pallas kernels for 19% -> 18%
where the time goes in v3:
time: 93.3 us; the launch traced here: 92.8 us
  waiting for transfers between devices  41.6 us (45%)
  Pallas kernels  25 us (27%)
  starting transfers between devices  18.9 us (20%)
  local copies, waits for them, and re-layouts  4.27 us (5%)
  matrix products  2.23 us (2%)
    all_to_all x1, waiting for transfers between devices, shards(): lax.all_to_all(copies_in, 'dp', split_axis=0, concat_axis=0, tiled=True)  39.9 us
    pallas_call x2, Pallas kernels, factor(): pl.pallas_call(functools.partial(factor_kernel, width, tile, 512, aligned...  23.8 us
    all_to_all x1, starting transfers between devices, shards(): lax.all_to_all(copies_grad, 'dp', split_axis=0, concat_axis=0, tiled=True)  11.5 us
    all_to_all x1, starting transfers between devices, shards(): lax.all_to_all(copies_in, 'dp', split_axis=0, concat_axis=0, tiled=True)  7.4 us
    unnamed x11, local copies, waits for them, and re-layouts  4.18 us
    dot_general x1, matrix products, shards(): jnp.einsum('gaws,gaf->wgsf', chosen, gradients.reshape(group_size, pair_r...  1.9 us
  transfers between devices with their start and end apart: 2, of which 2 were waited for; matrix products, arithmetic and copies ran while one was open for 3% of the time, Pallas kernels for 18%

profile of v3, /device:TPU:0, one launch (start us, length us, event | category | flops | bytes accessed | tf_op | source)
XLA Modules:
  0.0 92.8 jit_solution(16291289388010596102)
XLA Ops:
  0.6 0.0 copy-start
  0.6 0.9 %copy.7.ids_ref = s32[128,8]{1,0:T(8,128)S(1)} copy(s32[128,8]{0,1:T(8,128)} %param.6) | data formatting | bytes 8192 | tf_op args[2]
  1.6 0.0 copy-start.2
  1.6 1.2 %copy-done.2 = bf16[128,4096]{1,0:T(8,128)(2,1)S(1)} copy-done((bf16[128,4096]{1,0:T(8,128)(2,1)S(1)}, bf16[128,4096]{1,0:T(8,128)(2,1)}, u32[]{:S(2)}) %copy-start.2) | copy-done | bytes 1048600
  2.8 0.0 copy-start.3
  2.8 0.7 copy-done.3
  3.5 0.0 copy-start.4
  3.5 1.2 %select_rows.1 = bf16[256,4224]{1,0:T(8,128)(2,1)S(1)} custom-call(s32[128,8]{1,0:T(8,128)S(1)} %copy.7.ids_ref, s32[1,16]{1,0:T(1,128)S(1)} %bitcast.12, bf16[128,4096]{1,0:T(8,128)(2,1)S(1)} %copy-done.2), custom_call_target="tpu_custom_call" | custom-call | flops 268435456 | bytes 3145728 | tf_op jit(solution)/shard_map/select_rows/pallas_call | solution.py:117
  4.7 0.0 copy-start.1
  4.7 1.3 %copy-done.1 = bf16[256,4224]{1,0:T(8,128)(2,1)} copy-done((bf16[256,4224]{1,0:T(8,128)(2,1)}, bf16[256,4224]{1,0:T(8,128)(2,1)S(1)}, u32[]{:S(2)}) %copy-start.1) | copy-done | bytes 2162712
  6.1 7.4 %all-to-all-start = ((bf16[16,16,4224]{2,1,0:T(8,128)(2,1)}), bf16[16,16,4224]{2,1,0:T(8,128)(2,1)}, u32[]{:S(2)}, u32[]{:S(2)}) async-start(bf16[16,16,4224]{2,1,0:T(8,128)(2,1)} %bitcast.11), calls=%async_computation | async-start | bytes 4325376 | tf_op jit(solution)/shard_map/all_to_all | solution.py:189
  13.5 0.1 eq.52
  13.6 0.0 copy-done.4
  13.6 0.1 convert_compare_fusion
  13.7 0.3 fusion.6
  14.0 0.0 copy-done
  14.0 1.9 %fusion.3 = bf16[16,16,1536]{2,1,0:T(8,128)(2,1)} fusion(bf16[128,8,1536]{2,1,0:T(8,128)(2,1)S(1)} %copy-done, f32[1024,16]{0,1:T(8,128)S(1)} %fusion.6, pred[1024,16]{0,1:T(8,128)(4,1)S(1)} %convert_compare_fusion), kind=kOutput, calls=%fused_computation.4 | convolution fusion | flops 806223872 | bytes 4014080 | tf_op jit(solution)/shard_map/gaws,gaf->wgsf/dot_general | solution.py:177
  15.9 39.9 %all-to-all-done = bf16[16,16,4224]{2,1,0:T(8,128)(2,1)} async-done(((bf16[16,16,4224]{2,1,0:T(8,128)(2,1)}), bf16[16,16,4224]{2,1,0:T(8,128)(2,1)}, u32[]{:S(2)}, u32[]{:S(2)}) %all-to-all-start) | async-done | bytes 2162720 | tf_op jit(solution)/shard_map/all_to_all | solution.py:189
  55.8 11.5 %all-to-all-start.1 = ((bf16[16,16,1536]{2,1,0:T(8,128)(2,1)}), bf16[16,16,1536]{2,1,0:T(8,128)(2,1)}, u32[]{:S(2)}, u32[]{:S(2)}) async-start(bf16[16,16,1536]{2,1,0:T(8,128)(2,1)} %fusion.3), calls=%async_computation.1 | async-start | bytes 1572864 | tf_op jit(solution)/shard_map/all_to_all | solution.py:190
  67.3 17.0 %input_factor.1 = bf16[4096,4096]{1,0:T(8,128)(2,1)} custom-call(s32[1]{0:T(128)} %constant.21.clone.1.start_ref, bf16[256,4224]{1,0:T(8,128)(2,1)} %bitcast.2.flags_ref.left_ref.rows_ref, bf16[256,4224]{1,0:T(8,128)(2,1)} %bitcast.2.flags_ref.left_ref.rows_ref, bf16[256,4224]{1,0:T(8,128)(2,1)} %bitcast.2.flags_ref.left_ref.rows_ref), custom_call_target="tpu_custom_call" | custom-call | flops 8589934592 | bytes 35651584 | tf_op jit(solution)/shard_map/input_factor/pallas_call | solution.py:136
  84.3 1.7 %all-to-all-done.1 = bf16[16,16,1536]{2,1,0:T(8,128)(2,1)} async-done(((bf16[16,16,1536]{2,1,0:T(8,128)(2,1)}), bf16[16,16,1536]{2,1,0:T(8,128)(2,1)}, u32[]{:S(2)}, u32[]{:S(2)}) %all-to-all-start.1) | async-done | bytes 786464 | tf_op jit(solution)/shard_map/all_to_all | solution.py:190
  86.1 6.7 %grad_factor.1 = bf16[1536,1536]{1,0:T(8,128)(2,1)} custom-call(s32[1]{0:T(128)} %constant.21.clone.1.start_ref, bf16[256,4224]{1,0:T(8,128)(2,1)} %bitcast.2.flags_ref.left_ref.rows_ref, bf16[256,1536]{1,0:T(8,128)(2,1)} %bitcast.5.left_ref.rows_ref, bf16[256,1536]{1,0:T(8,128)(2,1)} %bitcast.5.left_ref.rows_ref), custom_call_target="tpu_custom_call" | custom-call | flops 1207959552 | bytes 5505024 | tf_op jit(solution)/shard_map/grad_factor/pallas_call | solution.py:136
Async XLA Ops:
  0.6 13.4 %copy-start = (bf16[128,8,1536]{2,1,0:T(8,128)(2,1)S(1)}, bf16[128,8,1536]{2,1,0:T(8,128)(2,1)}, u32[]{:S(2)}) copy-start(bf16[128,8,1536]{2,1,0:T(8,128)(2,1)} %param.5) | copy-start | bytes 9437188
  1.6 1.2 %copy-start.2 = (bf16[128,4096]{1,0:T(8,128)(2,1)S(1)}, bf16[128,4096]{1,0:T(8,128)(2,1)}, u32[]{:S(2)}) copy-start(bf16[128,4096]{1,0:T(8,128)(2,1)} %act_ref.1) | copy-start | bytes 3145732
  2.8 0.7 copy-start.3
  3.5 10.1 %copy-start.4 = (s32[16]{0:T(128)S(1)}, s32[16]{0:T(128)}, u32[]{:S(2)}) copy-start(s32[16]{0:T(128)} %param.7) | copy-start | bytes 196
  4.7 1.3 %copy-start.1 = (bf16[256,4224]{1,0:T(8,128)(2,1)}, bf16[256,4224]{1,0:T(8,128)(2,1)S(1)}, u32[]{:S(2)}) copy-start(bf16[256,4224]{1,0:T(8,128)(2,1)S(1)} %select_rows.1) | copy-start | bytes 6488068
  6.1 49.7 %all-to-all-start = ((bf16[16,16,4224]{2,1,0:T(8,128)(2,1)}), bf16[16,16,4224]{2,1,0:T(8,128)(2,1)}, u32[]{:S(2)}, u32[]{:S(2)}) async-start(bf16[16,16,4224]{2,1,0:T(8,128)(2,1)} %bitcast.11), calls=%async_computation | async-start | bytes 4325376 | tf_op jit(solution)/shard_map/all_to_all | solution.py:189
  55.8 30.3 %all-to-all-start.1 = ((bf16[16,16,1536]{2,1,0:T(8,128)(2,1)}), bf16[16,16,1536]{2,1,0:T(8,128)(2,1)}, u32[]{:S(2)}, u32[]{:S(2)}) async-start(bf16[16,16,1536]{2,1,0:T(8,128)(2,1)} %fusion.3), calls=%async_computation.1 | async-start | bytes 1572864 | tf_op jit(solution)/shard_map/all_to_all | solution.py:190

commit v4 on v2

--- a/solution.py
+++ b/solution.py
@@ -23,12 +23,13 @@
     return span
 
 
-def factor_kernel(width, tile, chunk, aligned, start_ref, flags_ref, left_ref, rows_ref, out_ref, scale_ref):
-    step = pl.program_id(0)
+def factor_kernel(width, tile, chunk, aligned, first, start_ref, flags_ref, left_ref, rows_ref, *rest):
+    out_ref, scale_ref = rest[-2:]
+    step = pl.program_id(0) + first
     depth = rows_ref.shape[0]
     piece = min(depth, 128)
 
-    @pl.when(step == 0)
+    @pl.when(step == first)
     def _():
         def add(i, sums):
             rows = pl.ds(pl.multiple_of(i * piece, piece), piece)
@@ -127,30 +128,50 @@
     )(expert_ids, window_experts.reshape(1, WIN), activations)
 
 
-def factor(rows, width, flagged, block_index, group_size, name):
+def factor(rows, width, flagged, block_index, group_size, name, part=(0, 1), held=None):
     depth = rows.shape[0]
     span = width // group_size
     tile = row_tile(span)
     aligned = group_size == 1
     left = rows if aligned else lax.dynamic_slice_in_dim(rows, block_index * span, span, 1)
+    steps = span // tile
+    first, last = part[0] * steps // part[1], (part[0] + 1) * steps // part[1]
     return pl.pallas_call(
-        functools.partial(factor_kernel, width, tile, 512, aligned),
+        functools.partial(factor_kernel, width, tile, 512, aligned, first),
         out_shape=jax.ShapeDtypeStruct((span, width), jnp.bfloat16),
-        grid=(span // tile,),
+        grid=(last - first,),
         in_specs=[
             pl.BlockSpec(memory_space=pltpu.SMEM),
             pl.BlockSpec((depth, FLAG), lambda i: (0, flagged.shape[1] // FLAG - 1)),
-            pl.BlockSpec((depth, tile), lambda i: (0, i)),
+            pl.BlockSpec((depth, tile), lambda i: (0, i + first)),
             pl.BlockSpec(rows.shape, lambda i: (0, 0)),
-        ],
-        out_specs=pl.BlockSpec((tile, width), lambda i: (i, 0)),
+        ] + [pl.BlockSpec(memory_space=pl.ANY)] * (held is not None),
+        input_output_aliases={} if held is None else {4: 0},
+        out_specs=pl.BlockSpec((tile, width), lambda i: (i + first, 0)),
         scratch_shapes=[pltpu.SMEM((2,), jnp.float32)],
         compiler_params=pltpu.CompilerParams(vmem_limit_bytes=56 * 1024 * 1024),
         cost_estimate=pl.CostEstimate(
-            flops=2 * depth * span * width, bytes_accessed=2 * span * width + 2 * depth * width, transcendentals=0
+            flops=2 * depth * (last - first) * tile * width, bytes_accessed=2 * (last - first) * tile * width + 2 * depth * width, transcendentals=0
         ),
         name=name,
-    )((block_index * span).astype(jnp.int32).reshape(1), flagged, left, rows)
+    )((block_index * span).astype(jnp.int32).reshape(1), flagged, left, rows, *([] if held is None else [held]))
+
+
+def stack_kernel(*refs):
+    depth = refs[0].shape[0]
+    for k, piece in enumerate(refs[:-1]):
+        refs[-1][k * depth:(k + 1) * depth, :] = piece[...]
+
+
+def stack(pieces):
+    depth, width = pieces[0].shape
+    return pl.pallas_call(
+        stack_kernel,
+        out_shape=jax.ShapeDtypeStruct((len(pieces) * depth, width), pieces[0].dtype),
+        in_specs=[pl.BlockSpec(memory_space=pltpu.VMEM)] * len(pieces),
+        out_specs=pl.BlockSpec(memory_space=pltpu.VMEM),
+        name="stack_rows",
+    )(*pieces)
 
 
 def shards(activations, gradients, expert_ids, window_experts):
@@ -183,13 +204,28 @@
     copies_in = jnp.repeat(
         in_sorted.reshape(WIN, group_size * slot_rows, width_in + FLAG), group_size, axis=0
     )
-    copies_grad = jnp.repeat(
-        grad_sorted.reshape(WIN, group_size * slot_rows, width_grad), group_size, axis=0
-    )
     in_rows = lax.all_to_all(copies_in, "dp", split_axis=0, concat_axis=0, tiled=True)
-    grad_rows = lax.all_to_all(copies_grad, "dp", split_axis=0, concat_axis=0, tiled=True)
     in_rows = in_rows.reshape(-1, width_in + FLAG)
-    grad_rows = grad_rows.reshape(-1, width_grad)
+    grad_blocks = grad_sorted.reshape(WIN, group_size * slot_rows, width_grad)
+    if group_size == 1:
+        me = lax.axis_index("dp")
+        sends = [lax.dynamic_index_in_dim(grad_blocks, me ^ k, 0, keepdims=False) for k in range(devices)]
+        in_rows, *sends = lax.optimization_barrier((in_rows, *sends))
+        landed, held, parts = [sends[0]], None, 3
+        sends = sends[1:]
+        share = -(-len(sends) // parts)
+        for part in range(parts):
+            in_rows, *ready = lax.optimization_barrier((in_rows, *landed, *sends[part * share:]))
+            landed, sends[part * share:] = list(ready[:len(landed)]), list(ready[len(landed):])
+            for k in range(part * share + 1, min(devices, (part + 1) * share + 1)):
+                landed.append(lax.ppermute(sends[k - 1], "dp", [(i, i ^ k) for i in range(devices)]))
+            held = factor(in_rows, width_in, in_rows, me * 0, 1, "input_factor", (part, parts), held)
+        grad_rows = stack(landed)
+        return held, factor(grad_rows, width_grad, in_rows, me * 0, 1, "grad_factor")
+    else:
+        copies_grad = jnp.repeat(grad_blocks, group_size, axis=0)
+        grad_rows = lax.all_to_all(copies_grad, "dp", split_axis=0, concat_axis=0, tiled=True)
+        grad_rows = grad_rows.reshape(-1, width_grad)
     block_index = lax.axis_index("dp") % group_size
     return (
         factor(in_rows, width_in, in_rows, block_index, group_size, "input_factor"),

time: 91.7 us -> 117 us (1.28)
  starting transfers between devices: 18.9 us -> 34.9 us
  Pallas kernels: 23.4 us -> 33 us
  waiting for transfers between devices: 41.6 us -> 39.8 us
  local copies, waits for them, and re-layouts: 4.27 us -> 5.8 us
    ppermute x0 -> x15, starting transfers between devices: none -> 27.5 us  [shards(): lax.ppermute(sends[k - 1], 'dp', [(i, i ^ k) for i in range(devices)])]
    all_to_all x1 -> x0, starting transfers between devices: 11.5 us -> none  [shards(): lax.all_to_all(copies_grad, 'dp', split_axis=0, concat_axis=0, tiled=True)]
    pallas_call x2 -> x4, Pallas kernels: 22.2 us -> 29.7 us  [factor(): pl.pallas_call(functools.partial(factor_kernel, width, tile, 512, aligned...]
    pallas_call x0 -> x1, Pallas kernels: none -> 2.06 us  [stack(): pl.pallas_call(stack_kernel, out_shape=jax.ShapeDtypeStruct((len(pieces)...]
    all_to_all x1 -> x0, waiting for transfers between devices: 1.75 us -> none  [shards(): lax.all_to_all(copies_grad, 'dp', split_axis=0, concat_axis=0, tiled=True)]
    unnamed x11 -> x49, local copies, waits for them, and re-layouts: 4.18 us -> 4.85 us
  transfers between devices with their start and end apart: 2 -> 16, of which waited for: 2 -> 1; matrix products, arithmetic and copies ran while one was open for 3% -> 2% of each run, Pallas kernels for 19% -> 21%
where the time goes in v4:
time: 117 us; the launch traced here: 116 us
  waiting for transfers between devices  39.8 us (34%)
  starting transfers between devices  34.9 us (30%)
  Pallas kernels  33 us (28%)
  local copies, waits for them, and re-layouts  5.8 us (5%)
  matrix products  1.31 us (1%)
    all_to_all x1, waiting for transfers between devices, shards(): lax.all_to_all(copies_in, 'dp', split_axis=0, concat_axis=0, tiled=True)  39.8 us
    pallas_call x4, Pallas kernels, factor(): pl.pallas_call(functools.partial(factor_kernel, width, tile, 512, aligned...  29.7 us
    ppermute x15, starting transfers between devices, shards(): lax.ppermute(sends[k - 1], 'dp', [(i, i ^ k) for i in range(devices)])  27.5 us
    all_to_all x1, starting transfers between devices, shards(): lax.all_to_all(copies_in, 'dp', split_axis=0, concat_axis=0, tiled=True)  7.4 us
    unnamed x49, local copies, waits for them, and re-layouts  4.85 us
  transfers between devices with their start and end apart: 16, of which 1 were waited for; matrix products, arithmetic and copies ran while one was open for 2% of the time, Pallas kernels for 21%

profile of v4, /device:TPU:0, one launch (start us, length us, event | category | flops | bytes accessed | tf_op | source)
XLA Modules:
  0.0 116.1 jit_solution(9834457085491792824)
XLA Ops:
  0.6 0.0 copy-start
  0.6 0.9 copy.9.ids_ref
  1.6 1.2 %copy-done.2 = bf16[128,4096]{1,0:T(8,128)(2,1)S(1)} copy-done((bf16[128,4096]{1,0:T(8,128)(2,1)S(1)}, bf16[128,4096]{1,0:T(8,128)(2,1)}, u32[]{:S(2)}) %copy-start.2) | copy-done | bytes 1048600
  2.8 0.7 copy-done.3
  3.5 1.2 %select_rows.1 = bf16[256,4224]{1,0:T(8,128)(2,1)S(1)} custom-call(s32[128,8]{1,0:T(8,128)S(1)} %copy.9.ids_ref, s32[1,16]{1,0:T(1,128)S(1)} %bitcast.139, bf16[128,4096]{1,0:T(8,128)(2,1)S(1)} %copy-done.2), custom_call_target="tpu_custom_call" | custom-call | flops 268435456 | bytes 3145728 | tf_op jit(solution)/shard_map/select_rows/pallas_call | solution.py:118
  4.7 0.0 copy-start.1
  4.7 1.3 %copy-done.1 = bf16[256,4224]{1,0:T(8,128)(2,1)} copy-done((bf16[256,4224]{1,0:T(8,128)(2,1)}, bf16[256,4224]{1,0:T(8,128)(2,1)S(1)}, u32[]{:S(2)}) %copy-start.1) | copy-done | bytes 2162712
  6.1 7.4 %all-to-all-start = ((bf16[16,16,4224]{2,1,0:T(8,128)(2,1)}), bf16[16,16,4224]{2,1,0:T(8,128)(2,1)}, u32[]{:S(2)}, u32[]{:S(2)}) async-start(bf16[16,16,4224]{2,1,0:T(8,128)(2,1)} %bitcast.138), calls=%async_computation | async-start | bytes 4325376 | tf_op jit(solution)/shard_map/all_to_all | solution.py:207
  13.6 0.1 eq.50
  13.7 0.0 copy-done.4
  13.7 0.1 convert_compare_fusion
  13.8 0.3 fusion.6
  14.2 0.0 copy-done
  14.2 1.0 fusion.3
  15.2 0.9 dynamic-slice_bitcast_fusion
  16.0 39.8 %all-to-all-done = bf16[16,16,4224]{2,1,0:T(8,128)(2,1)} async-done(((bf16[16,16,4224]{2,1,0:T(8,128)(2,1)}), bf16[16,16,4224]{2,1,0:T(8,128)(2,1)}, u32[]{:S(2)}, u32[]{:S(2)}) %all-to-all-start) | async-done | bytes 2162720 | tf_op jit(solution)/shard_map/all_to_all | solution.py:207
  55.8 0.0 copy-start.10
  55.8 0.8 collective-permute-start
  56.7 3.5 %collective-permute-start.1 = (bf16[16,1536]{1,0:T(8,128)(2,1)}, bf16[16,1536]{1,0:T(8,128)(2,1)S(1)}, u32[]{:S(2)}, u32[]{:S(2)}) collective-permute-start(bf16[16,1536]{1,0:T(8,128)(2,1)} %get-tuple-element.56), channel_id=1, source_target_pairs={{0,2},{1,3},{2,0},{3,1},{4,6},{5,7},{6,4},{7,5},{8,10},{9,11},{10,... | collective-permute-start | bytes 147464 | tf_op jit(solution)/shard_map/ppermute | solution.py:221
  60.1 0.0 collective-permute-start.2
  60.1 5.9 %collective-permute-start.3 = (bf16[16,1536]{1,0:T(8,128)(2,1)S(1)}, bf16[16,1536]{1,0:T(8,128)(2,1)S(1)}, u32[]{:S(2)}, u32[]{:S(2)}) collective-permute-start(bf16[16,1536]{1,0:T(8,128)(2,1)S(1)} %get-tuple-element.58), channel_id=1, source_target_pairs={{0,4},{1,5},{2,6},{3,7},{4,0},{5,1},{6,2},{7,3},{8,12},{9,13},{10,... | collective-permute-start | bytes 147464 | tf_op jit(solution)/shard_map/ppermute | solution.py:221
  66.0 0.0 collective-permute-start.4
  66.0 6.9 %input_factor.3.rest_0_ = bf16[4096,4096]{1,0:T(8,128)(2,1)} custom-call(s32[1]{0:T(128)} %constant.72.clone.1.start_ref, bf16[256,4224]{1,0:T(8,128)(2,1)} %bitcast.2.flags_ref.left_ref.rows_ref, bf16[256,4224]{1,0:T(8,128)(2,1)} %bitcast.2.flags_ref.left_ref.rows_ref, bf16[256,4224]{1,0:T(8,128)(2,1)} %bitcast.2.flags_ref.left_ref.rows_ref), custom_call_target="tpu_custom_call" | custom-call | flops 2147483648 | bytes 10485760 | tf_op jit(solution)/shard_map/input_factor/pallas_call | solution.py:139
  72.9 0.0 collective-permute-done.refs_1_
  72.9 0.0 collective-permute-done.1.refs_2_
  72.9 0.0 copy-start.6
  72.9 0.0 collective-permute-done.2.refs_3_
  72.9 0.0 copy-start.7
  72.9 0.0 collective-permute-done.3.refs_4_
  72.9 0.0 copy-start.8
  72.9 0.0 collective-permute-done.4.refs_5_
  72.9 3.0 %collective-permute-start.5 = (bf16[16,1536]{1,0:T(8,128)(2,1)S(1)}, bf16[16,1536]{1,0:T(8,128)(2,1)S(1)}, u32[]{:S(2)}, u32[]{:S(2)}) collective-permute-start(bf16[16,1536]{1,0:T(8,128)(2,1)S(1)} %copy-done.14), channel_id=1, source_target_pairs={{0,6},{1,7},{2,4},{3,5},{4,2},{5,3},{6,0},{7,1},{8,14},{9,15},{10,... | collective-permute-start | bytes 147464 | tf_op jit(solution)/shard_map/ppermute | solution.py:221
  75.9 0.0 copy-done.13
  75.9 0.0 collective-permute-start.6
  75.9 2.9 %collective-permute-start.7 = (bf16[16,1536]{1,0:T(8,128)(2,1)S(1)}, bf16[16,1536]{1,0:T(8,128)(2,1)S(1)}, u32[]{:S(2)}, u32[]{:S(2)}) collective-permute-start(bf16[16,1536]{1,0:T(8,128)(2,1)S(1)} %copy-done.12), channel_id=1, source_target_pairs={{0,8},{1,9},{2,10},{3,11},{4,12},{5,13},{6,14},{7,15},{8,0},{9,1},... | collective-permute-start | bytes 147464 | tf_op jit(solution)/shard_map/ppermute | solution.py:221
  78.8 0.0 copy-done.11
  78.8 0.0 collective-permute-start.8
  78.8 2.1 %collective-permute-start.9 = (bf16[16,1536]{1,0:T(8,128)(2,1)S(1)}, bf16[16,1536]{1,0:T(8,128)(2,1)S(1)}, u32[]{:S(2)}, u32[]{:S(2)}) collective-permute-start(bf16[16,1536]{1,0:T(8,128)(2,1)S(1)} %copy-done.10), channel_id=1, source_target_pairs={{0,10},{1,11},{2,8},{3,9},{4,14},{5,15},{6,12},{7,13},{8,2},{9,3},... | collective-permute-start | bytes 147464 | tf_op jit(solution)/shard_map/ppermute | solution.py:221
  81.0 8.8 %input_factor.4.rest_0_ = bf16[4096,4096]{1,0:T(8,128)(2,1)} custom-call(s32[1]{0:T(128)} %constant.72.clone.1.start_ref, bf16[256,4224]{1,0:T(8,128)(2,1)} %bitcast.2.flags_ref.left_ref.rows_ref, bf16[256,4224]{1,0:T(8,128)(2,1)} %bitcast.2.flags_ref.left_ref.rows_ref, ...), custom_call_target="tpu_custom_call", output_to_operand_aliasing={{}: (4, {})} | custom-call | flops 3221225472 | bytes 14680064 | tf_op jit(solution)/shard_map/input_factor/pallas_call | solution.py:139
  89.8 0.0 copy-done.7
  89.8 0.0 collective-permute-done.5.refs_6_
  89.9 0.0 collective-permute-done.6.refs_7_
  89.9 0.0 collective-permute-done.7.refs_8_
  89.9 0.0 copy-start.17
  89.9 0.0 collective-permute-done.8.refs_9_
  89.9 0.0 collective-permute-done.9.refs_10_
  89.9 1.3 %collective-permute-start.10 = (bf16[16,1536]{1,0:T(8,128)(2,1)S(1)}, bf16[16,1536]{1,0:T(8,128)(2,1)S(1)}, u32[]{:S(2)}, u32[]{:S(2)}) collective-permute-start(bf16[16,1536]{1,0:T(8,128)(2,1)S(1)} %get-tuple-element.99), channel_id=1, source_target_pairs={{0,11},{1,10},{2,9},{3,8},{4,15},{5,14},{6,13},{7,12},{8,3},{9,2},... | collective-permute-start | bytes 147464 | tf_op jit(solution)/shard_map/ppermute | solution.py:221
  91.3 2.3 %collective-permute-start.11 = (bf16[16,1536]{1,0:T(8,128)(2,1)S(1)}, bf16[16,1536]{1,0:T(8,128)(2,1)S(1)}, u32[]{:S(2)}, u32[]{:S(2)}) collective-permute-start(bf16[16,1536]{1,0:T(8,128)(2,1)S(1)} %get-tuple-element.100), channel_id=1, source_target_pairs={{0,12},{1,13},{2,14},{3,15},{4,8},{5,9},{6,10},{7,11},{8,4},{9,5},... | collective-permute-start | bytes 147464 | tf_op jit(solution)/shard_map/ppermute | solution.py:221
  93.5 1.5 %collective-permute-start.12 = (bf16[16,1536]{1,0:T(8,128)(2,1)S(1)}, bf16[16,1536]{1,0:T(8,128)(2,1)S(1)}, u32[]{:S(2)}, u32[]{:S(2)}) collective-permute-start(bf16[16,1536]{1,0:T(8,128)(2,1)S(1)} %get-tuple-element.101), channel_id=1, source_target_pairs={{0,13},{1,12},{2,15},{3,14},{4,9},{5,8},{6,11},{7,10},{8,5},{9,4},... | collective-permute-start | bytes 147464 | tf_op jit(solution)/shard_map/ppermute | solution.py:221
  95.0 3.2 %collective-permute-start.13 = (bf16[16,1536]{1,0:T(8,128)(2,1)S(1)}, bf16[16,1536]{1,0:T(8,128)(2,1)S(1)}, u32[]{:S(2)}, u32[]{:S(2)}) collective-permute-start(bf16[16,1536]{1,0:T(8,128)(2,1)S(1)} %get-tuple-element.102), channel_id=1, source_target_pairs={{0,14},{1,15},{2,12},{3,13},{4,10},{5,11},{6,8},{7,9},{8,6},{9,7},... | collective-permute-start | bytes 147464 | tf_op jit(solution)/shard_map/ppermute | solution.py:221
  98.2 1.0 collective-permute-start.14
  99.2 8.8 %input_factor.5 = bf16[4096,4096]{1,0:T(8,128)(2,1)} custom-call(s32[1]{0:T(128)} %constant.72.clone.1.start_ref, bf16[256,4224]{1,0:T(8,128)(2,1)} %bitcast.2.flags_ref.left_ref.rows_ref, bf16[256,4224]{1,0:T(8,128)(2,1)} %bitcast.2.flags_ref.left_ref.rows_ref, ...), custom_call_target="tpu_custom_call", output_to_operand_aliasing={{}: (4, {})} | custom-call | flops 3221225472 | bytes 14680064 | tf_op jit(solution)/shard_map/input_factor/pallas_call | solution.py:139
  108.1 0.0 copy-done.18
  108.1 0.0 copy-done.19
  108.1 0.0 collective-permute-done.10.refs_11_
  108.1 0.0 collective-permute-done.11.refs_12_
  108.2 0.0 collective-permute-done.12.refs_13_
  108.2 0.0 copy-start.22
  108.2 0.0 collective-permute-done.13.refs_14_
  108.2 0.6 copy-done.23
  108.8 0.0 collective-permute-done.14.refs_15_
  108.8 0.0 copy-done.21
  108.8 2.1 %stack_rows.1.left_ref.rows_ref = bf16[256,1536]{1,0:T(8,128)(2,1)} custom-call(bf16[16,1536]{1,0:T(8,128)(2,1)} %get-tuple-element.88.refs_0_, bf16[16,1536]{1,0:T(8,128)(2,1)} %copy-done.5, bf16[16,1536]{1,0:T(8,128)(2,1)} %copy-done.6, bf16[16,1536]{1,0:T(8,128)(2,1)} %copy-done.7, bf16[16,1536]{1,0:T(8,128)(2,1)} %copy-done.8, ...), custom_call_target="tpu_custom_call" | custom-call | tf_op jit(solution)/shard_map/stack_rows/pallas_call | solution.py:168
  110.9 5.2 %grad_factor.1 = bf16[1536,1536]{1,0:T(8,128)(2,1)} custom-call(s32[1]{0:T(128)} %constant.72.clone.1.start_ref, bf16[256,4224]{1,0:T(8,128)(2,1)} %bitcast.2.flags_ref.left_ref.rows_ref, bf16[256,1536]{1,0:T(8,128)(2,1)} %stack_rows.1.left_ref.rows_ref, bf16[256,1536]{1,0:T(8,128)(2,1)} %stack_rows.1.left_ref.rows_ref), custom_call_target="tpu_custom_call" | custom-call | flops 1207959552 | bytes 5505024 | tf_op jit(solution)/shard_map/grad_factor/pallas_call | solution.py:139
  (28 shorter events, 0.1 us)
Async XLA Ops:
  0.6 13.5 %copy-start = (bf16[128,8,1536]{2,1,0:T(8,128)(2,1)S(1)}, bf16[128,8,1536]{2,1,0:T(8,128)(2,1)}, u32[]{:S(2)}) copy-start(bf16[128,8,1536]{2,1,0:T(8,128)(2,1)} %param.5) | copy-start | bytes 9437188
  1.6 1.2 %copy-start.2 = (bf16[128,4096]{1,0:T(8,128)(2,1)S(1)}, bf16[128,4096]{1,0:T(8,128)(2,1)}, u32[]{:S(2)}) copy-start(bf16[128,4096]{1,0:T(8,128)(2,1)} %act_ref.1) | copy-start | bytes 3145732
  2.8 0.7 copy-start.3
  3.5 10.3 %copy-start.4 = (s32[16]{0:T(128)S(1)}, s32[16]{0:T(128)}, u32[]{:S(2)}) copy-start(s32[16]{0:T(128)} %param.7) | copy-start | bytes 196
  4.7 1.3 %copy-start.1 = (bf16[256,4224]{1,0:T(8,128)(2,1)}, bf16[256,4224]{1,0:T(8,128)(2,1)S(1)}, u32[]{:S(2)}) copy-start(bf16[256,4224]{1,0:T(8,128)(2,1)S(1)} %select_rows.1) | copy-start | bytes 6488068
  6.1 49.7 %all-to-all-start = ((bf16[16,16,4224]{2,1,0:T(8,128)(2,1)}), bf16[16,16,4224]{2,1,0:T(8,128)(2,1)}, u32[]{:S(2)}, u32[]{:S(2)}) async-start(bf16[16,16,4224]{2,1,0:T(8,128)(2,1)} %bitcast.138), calls=%async_computation | async-start | bytes 4325376 | tf_op jit(solution)/shard_map/all_to_all | solution.py:207
  55.8 17.1 %copy-start.14 = (bf16[16,1536]{1,0:T(8,128)(2,1)S(1)}, bf16[16,1536]{1,0:T(8,128)(2,1)}, u32[]{:S(2)}) copy-start(bf16[16,1536]{1,0:T(8,128)(2,1)} %get-tuple-element.77) | copy-start | bytes 147460
  55.8 20.1 %copy-start.13 = (bf16[16,1536]{1,0:T(8,128)(2,1)S(1)}, bf16[16,1536]{1,0:T(8,128)(2,1)}, u32[]{:S(2)}) copy-start(bf16[16,1536]{1,0:T(8,128)(2,1)} %get-tuple-element.78) | copy-start | bytes 147460
  55.8 20.1 %copy-start.12 = (bf16[16,1536]{1,0:T(8,128)(2,1)S(1)}, bf16[16,1536]{1,0:T(8,128)(2,1)}, u32[]{:S(2)}) copy-start(bf16[16,1536]{1,0:T(8,128)(2,1)} %get-tuple-element.79) | copy-start | bytes 147460
  55.8 23.0 %copy-start.11 = (bf16[16,1536]{1,0:T(8,128)(2,1)S(1)}, bf16[16,1536]{1,0:T(8,128)(2,1)}, u32[]{:S(2)}) copy-start(bf16[16,1536]{1,0:T(8,128)(2,1)} %get-tuple-element.80) | copy-start | bytes 147460
  55.8 23.0 %copy-start.10 = (bf16[16,1536]{1,0:T(8,128)(2,1)S(1)}, bf16[16,1536]{1,0:T(8,128)(2,1)}, u32[]{:S(2)}) copy-start(bf16[16,1536]{1,0:T(8,128)(2,1)} %get-tuple-element.81) | copy-start | bytes 147460
  55.8 17.0 %collective-permute-start = (bf16[16,1536]{1,0:T(8,128)(2,1)}, bf16[16,1536]{1,0:T(8,128)(2,1)S(1)}, u32[]{:S(2)}, u32[]{:S(2)}) collective-permute-start(bf16[16,1536]{1,0:T(8,128)(2,1)} %get-tuple-element.55), channel_id=1, source_target_pairs={{0,1},{1,0},{2,3},{3,2},{4,5},{5,4},{6,7},{7,6},{8,9},{9,8},{10,11... | collective-permute-start | bytes 147464 | tf_op jit(solution)/shard_map/ppermute | solution.py:221
  56.7 16.2 %collective-permute-start.1 = (bf16[16,1536]{1,0:T(8,128)(2,1)}, bf16[16,1536]{1,0:T(8,128)(2,1)S(1)}, u32[]{:S(2)}, u32[]{:S(2)}) collective-permute-start(bf16[16,1536]{1,0:T(8,128)(2,1)} %get-tuple-element.56), channel_id=1, source_target_pairs={{0,2},{1,3},{2,0},{3,1},{4,6},{5,7},{6,4},{7,5},{8,10},{9,11},{10,... | collective-permute-start | bytes 147464 | tf_op jit(solution)/shard_map/ppermute | solution.py:221
  60.1 12.8 %collective-permute-start.2 = (bf16[16,1536]{1,0:T(8,128)(2,1)S(1)}, bf16[16,1536]{1,0:T(8,128)(2,1)S(1)}, u32[]{:S(2)}, u32[]{:S(2)}) collective-permute-start(bf16[16,1536]{1,0:T(8,128)(2,1)S(1)} %get-tuple-element.57), channel_id=1, source_target_pairs={{0,3},{1,2},{2,1},{3,0},{4,7},{5,6},{6,5},{7,4},{8,11},{9,10},{10,... | collective-permute-start | bytes 147464 | tf_op jit(solution)/shard_map/ppermute | solution.py:221
  60.1 12.8 %collective-permute-start.3 = (bf16[16,1536]{1,0:T(8,128)(2,1)S(1)}, bf16[16,1536]{1,0:T(8,128)(2,1)S(1)}, u32[]{:S(2)}, u32[]{:S(2)}) collective-permute-start(bf16[16,1536]{1,0:T(8,128)(2,1)S(1)} %get-tuple-element.58), channel_id=1, source_target_pairs={{0,4},{1,5},{2,6},{3,7},{4,0},{5,1},{6,2},{7,3},{8,12},{9,13},{10,... | collective-permute-start | bytes 147464 | tf_op jit(solution)/shard_map/ppermute | solution.py:221
  66.0 6.9 %collective-permute-start.4 = (bf16[16,1536]{1,0:T(8,128)(2,1)S(1)}, bf16[16,1536]{1,0:T(8,128)(2,1)S(1)}, u32[]{:S(2)}, u32[]{:S(2)}) collective-permute-start(bf16[16,1536]{1,0:T(8,128)(2,1)S(1)} %get-tuple-element.59), channel_id=1, source_target_pairs={{0,5},{1,4},{2,7},{3,6},{4,1},{5,0},{6,3},{7,2},{8,13},{9,12},{10,... | collective-permute-start | bytes 147464 | tf_op jit(solution)/shard_map/ppermute | solution.py:221
  72.9 16.9 %copy-start.5 = (bf16[16,1536]{1,0:T(8,128)(2,1)}, bf16[16,1536]{1,0:T(8,128)(2,1)S(1)}, u32[]{:S(2)}) copy-start(bf16[16,1536]{1,0:T(8,128)(2,1)S(1)} %collective-permute-done.refs_1_) | copy-start | bytes 147460
  72.9 16.9 %copy-start.6 = (bf16[16,1536]{1,0:T(8,128)(2,1)}, bf16[16,1536]{1,0:T(8,128)(2,1)S(1)}, u32[]{:S(2)}) copy-start(bf16[16,1536]{1,0:T(8,128)(2,1)S(1)} %collective-permute-done.1.refs_2_) | copy-start | bytes 147460
  72.9 16.9 %copy-start.7 = (bf16[16,1536]{1,0:T(8,128)(2,1)}, bf16[16,1536]{1,0:T(8,128)(2,1)S(1)}, u32[]{:S(2)}) copy-start(bf16[16,1536]{1,0:T(8,128)(2,1)S(1)} %collective-permute-done.2.refs_3_) | copy-start | bytes 147460
  72.9 16.9 %copy-start.8 = (bf16[16,1536]{1,0:T(8,128)(2,1)}, bf16[16,1536]{1,0:T(8,128)(2,1)S(1)}, u32[]{:S(2)}) copy-start(bf16[16,1536]{1,0:T(8,128)(2,1)S(1)} %collective-permute-done.3.refs_4_) | copy-start | bytes 147460
  72.9 16.9 %copy-start.9 = (bf16[16,1536]{1,0:T(8,128)(2,1)}, bf16[16,1536]{1,0:T(8,128)(2,1)S(1)}, u32[]{:S(2)}) copy-start(bf16[16,1536]{1,0:T(8,128)(2,1)S(1)} %collective-permute-done.4.refs_5_) | copy-start | bytes 147460
  72.9 16.9 %collective-permute-start.5 = (bf16[16,1536]{1,0:T(8,128)(2,1)S(1)}, bf16[16,1536]{1,0:T(8,128)(2,1)S(1)}, u32[]{:S(2)}, u32[]{:S(2)}) collective-permute-start(bf16[16,1536]{1,0:T(8,128)(2,1)S(1)} %copy-done.14), channel_id=1, source_target_pairs={{0,6},{1,7},{2,4},{3,5},{4,2},{5,3},{6,0},{7,1},{8,14},{9,15},{10,... | collective-permute-start | bytes 147464 | tf_op jit(solution)/shard_map/ppermute | solution.py:221
  75.9 13.9 %collective-permute-start.6 = (bf16[16,1536]{1,0:T(8,128)(2,1)S(1)}, bf16[16,1536]{1,0:T(8,128)(2,1)S(1)}, u32[]{:S(2)}, u32[]{:S(2)}) collective-permute-start(bf16[16,1536]{1,0:T(8,128)(2,1)S(1)} %copy-done.13), channel_id=1, source_target_pairs={{0,7},{1,6},{2,5},{3,4},{4,3},{5,2},{6,1},{7,0},{8,15},{9,14},{10,... | collective-permute-start | bytes 147464 | tf_op jit(solution)/shard_map/ppermute | solution.py:221
  75.9 13.9 %collective-permute-start.7 = (bf16[16,1536]{1,0:T(8,128)(2,1)S(1)}, bf16[16,1536]{1,0:T(8,128)(2,1)S(1)}, u32[]{:S(2)}, u32[]{:S(2)}) collective-permute-start(bf16[16,1536]{1,0:T(8,128)(2,1)S(1)} %copy-done.12), channel_id=1, source_target_pairs={{0,8},{1,9},{2,10},{3,11},{4,12},{5,13},{6,14},{7,15},{8,0},{9,1},... | collective-permute-start | bytes 147464 | tf_op jit(solution)/shard_map/ppermute | solution.py:221
  78.8 11.1 %collective-permute-start.8 = (bf16[16,1536]{1,0:T(8,128)(2,1)S(1)}, bf16[16,1536]{1,0:T(8,128)(2,1)S(1)}, u32[]{:S(2)}, u32[]{:S(2)}) collective-permute-start(bf16[16,1536]{1,0:T(8,128)(2,1)S(1)} %copy-done.11), channel_id=1, source_target_pairs={{0,9},{1,8},{2,11},{3,10},{4,13},{5,12},{6,15},{7,14},{8,1},{9,0},... | collective-permute-start | bytes 147464 | tf_op jit(solution)/shard_map/ppermute | solution.py:221
  78.8 11.1 %collective-permute-start.9 = (bf16[16,1536]{1,0:T(8,128)(2,1)S(1)}, bf16[16,1536]{1,0:T(8,128)(2,1)S(1)}, u32[]{:S(2)}, u32[]{:S(2)}) collective-permute-start(bf16[16,1536]{1,0:T(8,128)(2,1)S(1)} %copy-done.10), channel_id=1, source_target_pairs={{0,10},{1,11},{2,8},{3,9},{4,14},{5,15},{6,12},{7,13},{8,2},{9,3},... | collective-permute-start | bytes 147464 | tf_op jit(solution)/shard_map/ppermute | solution.py:221
  89.8 18.2 %copy-start.15 = (bf16[16,1536]{1,0:T(8,128)(2,1)}, bf16[16,1536]{1,0:T(8,128)(2,1)S(1)}, u32[]{:S(2)}) copy-start(bf16[16,1536]{1,0:T(8,128)(2,1)S(1)} %collective-permute-done.5.refs_6_) | copy-start | bytes 147460
  89.9 18.2 %copy-start.16 = (bf16[16,1536]{1,0:T(8,128)(2,1)}, bf16[16,1536]{1,0:T(8,128)(2,1)S(1)}, u32[]{:S(2)}) copy-start(bf16[16,1536]{1,0:T(8,128)(2,1)S(1)} %collective-permute-done.6.refs_7_) | copy-start | bytes 147460
  89.9 18.2 %copy-start.17 = (bf16[16,1536]{1,0:T(8,128)(2,1)}, bf16[16,1536]{1,0:T(8,128)(2,1)S(1)}, u32[]{:S(2)}) copy-start(bf16[16,1536]{1,0:T(8,128)(2,1)S(1)} %collective-permute-done.7.refs_8_) | copy-start | bytes 147460
  89.9 18.2 %copy-start.18 = (bf16[16,1536]{1,0:T(8,128)(2,1)}, bf16[16,1536]{1,0:T(8,128)(2,1)S(1)}, u32[]{:S(2)}) copy-start(bf16[16,1536]{1,0:T(8,128)(2,1)S(1)} %collective-permute-done.8.refs_9_) | copy-start | bytes 147460
  89.9 18.2 %copy-start.19 = (bf16[16,1536]{1,0:T(8,128)(2,1)}, bf16[16,1536]{1,0:T(8,128)(2,1)S(1)}, u32[]{:S(2)}) copy-start(bf16[16,1536]{1,0:T(8,128)(2,1)S(1)} %collective-permute-done.9.refs_10_) | copy-start | bytes 147460
  89.9 18.2 %collective-permute-start.10 = (bf16[16,1536]{1,0:T(8,128)(2,1)S(1)}, bf16[16,1536]{1,0:T(8,128)(2,1)S(1)}, u32[]{:S(2)}, u32[]{:S(2)}) collective-permute-start(bf16[16,1536]{1,0:T(8,128)(2,1)S(1)} %get-tuple-element.99), channel_id=1, source_target_pairs={{0,11},{1,10},{2,9},{3,8},{4,15},{5,14},{6,13},{7,12},{8,3},{9,2},... | collective-permute-start | bytes 147464 | tf_op jit(solution)/shard_map/ppermute | solution.py:221
  91.3 16.9 %collective-permute-start.11 = (bf16[16,1536]{1,0:T(8,128)(2,1)S(1)}, bf16[16,1536]{1,0:T(8,128)(2,1)S(1)}, u32[]{:S(2)}, u32[]{:S(2)}) collective-permute-start(bf16[16,1536]{1,0:T(8,128)(2,1)S(1)} %get-tuple-element.100), channel_id=1, source_target_pairs={{0,12},{1,13},{2,14},{3,15},{4,8},{5,9},{6,10},{7,11},{8,4},{9,5},... | collective-permute-start | bytes 147464 | tf_op jit(solution)/shard_map/ppermute | solution.py:221
  93.5 14.6 %collective-permute-start.12 = (bf16[16,1536]{1,0:T(8,128)(2,1)S(1)}, bf16[16,1536]{1,0:T(8,128)(2,1)S(1)}, u32[]{:S(2)}, u32[]{:S(2)}) collective-permute-start(bf16[16,1536]{1,0:T(8,128)(2,1)S(1)} %get-tuple-element.101), channel_id=1, source_target_pairs={{0,13},{1,12},{2,15},{3,14},{4,9},{5,8},{6,11},{7,10},{8,5},{9,4},... | collective-permute-start | bytes 147464 | tf_op jit(solution)/shard_map/ppermute | solution.py:221
  95.0 13.2 %collective-permute-start.13 = (bf16[16,1536]{1,0:T(8,128)(2,1)S(1)}, bf16[16,1536]{1,0:T(8,128)(2,1)S(1)}, u32[]{:S(2)}, u32[]{:S(2)}) collective-permute-start(bf16[16,1536]{1,0:T(8,128)(2,1)S(1)} %get-tuple-element.102), channel_id=1, source_target_pairs={{0,14},{1,15},{2,12},{3,13},{4,10},{5,11},{6,8},{7,9},{8,6},{9,7},... | collective-permute-start | bytes 147464 | tf_op jit(solution)/shard_map/ppermute | solution.py:221
  98.2 10.6 %collective-permute-start.14 = (bf16[16,1536]{1,0:T(8,128)(2,1)S(1)}, bf16[16,1536]{1,0:T(8,128)(2,1)}, u32[]{:S(2)}, u32[]{:S(2)}) collective-permute-start(bf16[16,1536]{1,0:T(8,128)(2,1)S(1)} %get-tuple-element.103), channel_id=1, source_target_pairs={{0,15},{1,14},{2,13},{3,12},{4,11},{5,10},{6,9},{7,8},{8,7},{9,6},... | collective-permute-start | bytes 147464 | tf_op jit(solution)/shard_map/ppermute | solution.py:221
  108.1 0.7 copy-start.20
  108.1 0.7 copy-start.21
  108.2 0.6 copy-start.22
  108.2 0.6 copy-start.23
